TPU v7x, 128 devices: a whole 4x4x4 slice. The times are simulated.
128 devices in a mesh: period: 4 (over x_hi, core), slab: 32 (over y, z, x_lo).
Axes of the slice: x: 4 (x_hi: 2, x_lo: 2; x = x_hi * 2 + x_lo), y: 4, z: 4, core: 2. Of those that a mesh axis runs over, the one named last changes fastest.
Arguments:
- final_window_dual_level: float32 [512, 16, 1024], P('slab'), may hold values from -6 to 6
- misfit: float32 [4, 512, 16, 1024], P('period', 'slab'), may hold values from -1.8 to 1.8
- conductivity: float32 [512, 16, 1024], P('slab'), may hold values from 0.3 to 3
- capacity: float32 [512, 16, 1024], P('slab'), may hold values from 0.005 to 0.05
- wells: int32 [1024], replicated, may hold values from 0 to 8388607
- plan: int32 [4, 1024], P('period'), may hold values 0 or 1
Outputs:
- corrected: float32 [4, 512, 16, 1024], P('period', 'slab')
- well_grad: float32 [1024], replicated
Inputs may be any that keep to these rules, and one draw needn't show every extreme that they name: wells[w] = (x * 16 + z) * 1024 + y for the cell of well w.
All inputs are finite; a program needn't handle non-finite values. No bound on the sum of `plan` on one device may be relied on, other than what follows from the above.
Results may differ from a plain program's by a relative error of at most 0.0001.
Values sent between devices are 32-bit elements; how exact they have to be, the bound alone decides.
A program may use at most 128 MiB of HBM per device.

v0:
```python
import jax
import jax.numpy as jnp
from jax import lax
from jax.sharding import PartitionSpec as P

STEPS = 2
SWEEPS = 8
CF = 16


def passed_along(array, axis, by):
    peers = lax.axis_size(axis)
    pairs = [(i, i + by) for i in range(peers) if 0 <= i + by < peers]
    return lax.ppermute(array, axis, pairs)


def with_halo(array, sides, width):
    for axis, dim in sides:
        peers, length = (lax.axis_size(axis), array.shape[dim])
        up = [(i, (i + 1) % peers) for i in range(peers - 1)]
        down = [(j, i) for i, j in up]
        last = lax.slice_in_dim(array, length - width, length, axis=dim)
        first = lax.slice_in_dim(array, 0, width, axis=dim)
        before = lax.ppermute(last, axis, up)
        after = lax.ppermute(first, axis, down)
        array = jnp.concatenate([before, array, after], axis=dim)
    return array


def below_y(array_in):
    return jnp.pad(array_in, ((0, 0), (0, 0), (1, 0)))[:, :, :-1]


def above_y(array_in):
    return jnp.pad(array_in, ((0, 0), (0, 0), (0, 1)))[:, :, 1:]


def below_z(array_in):
    return jnp.pad(array_in, ((0, 0), (1, 0), (0, 0)))[:, :-1, :]


def above_z(array_in):
    return jnp.pad(array_in, ((0, 0), (0, 1), (0, 0)))[:, 1:, :]


def face_table(widened, z_scale):
    middle = widened[1:-1]
    return (
        jnp.sqrt(middle * widened[:-2]),
        jnp.sqrt(middle * widened[2:]),
        jnp.sqrt(middle * below_y(middle)),
        jnp.sqrt(middle * above_y(middle)),
        z_scale * jnp.sqrt(middle * below_z(middle)),
        z_scale * jnp.sqrt(middle * above_z(middle)),
    )


def inverse_diagonal(storage, transmit):
    return 1.0 / (
        storage + transmit[0] + transmit[1] + transmit[2] + transmit[3] + transmit[4] + transmit[5]
    )


def relax(row_below, row_centre, row_above, source, transmit, inverse):
    nearby = transmit[0] * row_below + transmit[1] * row_above
    nearby = nearby + transmit[2] * below_y(row_centre) + transmit[3] * above_y(row_centre)
    nearby = nearby + transmit[4] * below_z(row_centre) + transmit[5] * above_z(row_centre)
    return (source + nearby) * inverse


def restrict(array_in):
    height, layers, across = array_in.shape
    return array_in.reshape(height // CF, CF, layers, across // CF, CF).mean(axis=(1, 4))


def extend_level_map(coarse):
    return jnp.repeat(jnp.repeat(coarse, CF, axis=0), CF, axis=2)


def predicted_solution_list(
    rough_evolution_operator, closing_solution, highest_team_flag, number_of_teams
):
    guessed_solution = jnp.where(
        highest_team_flag, closing_solution, jnp.zeros_like(closing_solution)
    )
    stepped_solution = rough_evolution_operator(guessed_solution)
    for _ in range(number_of_teams - 1):
        incoming_solution = passed_along(stepped_solution, "period", -1)
        guessed_solution = jnp.where(highest_team_flag, closing_solution, incoming_solution)
        stepped_solution = rough_evolution_operator(guessed_solution)
    return (guessed_solution, stepped_solution)


def correction_chain(rough_evolution_operator, jump_term, number_of_teams):
    carry_value = jump_term
    for _ in range(number_of_teams - 1):
        incoming_solution = passed_along(carry_value, "period", -1)
        carry_value = jump_term + rough_evolution_operator(incoming_solution)
    return carry_value


def shards(final_window_dual_level, misfit, conductivity, capacity, wells, plan):
    number_of_teams = lax.axis_size("period")
    team_rank = lax.axis_index("period")
    highest_team_flag = team_rank == number_of_teams - 1
    height, layers, across = final_window_dual_level.shape
    periods_here = misfit.shape[0]
    widened = with_halo(conductivity, (("slab", 0),), 1)
    transmit = face_table(widened, 1.0)
    inverse = inverse_diagonal(capacity, transmit)

    def fine_step(dual_piezometric_level, period):
        forcing = lax.dynamic_index_in_dim(misfit, period, 0, keepdims=False)
        own_rhs = capacity * dual_piezometric_level + forcing
        current = dual_piezometric_level
        for _ in range(SWEEPS):
            outer = with_halo(current, (("slab", 0),), 1)
            current = relax(outer[:-2], current, outer[2:], own_rhs, transmit, inverse)
        return current

    coarse_cond = restrict(conductivity)
    coarse_store = restrict(capacity) * (CF * CF / (STEPS * periods_here))
    closing_solution = restrict(final_window_dual_level)
    coarse_wide = with_halo(coarse_cond, (("slab", 0),), 1)
    coarse_transmit = face_table(coarse_wide, float(CF * CF))
    coarse_inverse = inverse_diagonal(coarse_store, coarse_transmit)

    def rough_evolution_operator(local_state):
        source = coarse_store * local_state
        current = local_state
        for _ in range(SWEEPS):
            outer = with_halo(current, (("slab", 0),), 1)
            current = relax(outer[:-2], current, outer[2:], source, coarse_transmit, coarse_inverse)
        return current

    guessed_solution, stepped_solution = predicted_solution_list(
        rough_evolution_operator, closing_solution, highest_team_flag, number_of_teams
    )
    starting_level_map = jnp.where(
        highest_team_flag, final_window_dual_level, extend_level_map(guessed_solution)
    )
    local_cells = height * layers * across
    local_wells = wells - lax.axis_index("slab") * local_cells
    owned_mask = ((local_wells >= 0) & (local_wells < local_cells)).astype(jnp.float32)
    safe_index = jnp.clip(local_wells, 0, local_cells - 1)

    def advance(turn_index, carried):
        dual_piezometric_level, totals = carried
        period = periods_here - 1 - turn_index // STEPS
        dual_piezometric_level = fine_step(dual_piezometric_level, period)
        active = lax.dynamic_index_in_dim(plan, period, 0, keepdims=False).astype(jnp.float32)
        sampled = jnp.take(dual_piezometric_level.reshape(-1), safe_index) * owned_mask
        return (dual_piezometric_level, totals + active * sampled)

    ending, totals = lax.fori_loop(
        0, STEPS * periods_here, advance, (starting_level_map, jnp.zeros(wells.shape, jnp.float32))
    )
    jump_term = restrict(ending) - stepped_solution
    carry_value = correction_chain(rough_evolution_operator, jump_term, number_of_teams)
    corrected = ending + extend_level_map(carry_value - jump_term)
    grand_total = lax.psum(totals, ("period", "slab"))
    return (corrected[None], grand_total / (STEPS * periods_here * number_of_teams))


def solution(mesh):
    return jax.shard_map(
        shards,
        mesh=mesh,
        in_specs=(
            P("slab", None, None),
            P("period", "slab", None, None),
            P("slab", None, None),
            P("slab", None, None),
            P(),
            P("period", None),
        ),
        out_specs=(P("period", "slab", None, None), P()),
        check_vma=False,
    )
```

profile of v0, /device:TPU:0, one launch (start us, length us, event | category | flops | bytes accessed | tf_op | source)
XLA Modules:
  0.0 1014.4 jit_solution(1892616354606933824)
XLA Ops:
  13.9 8.4 add_divide_fusion
  24.6 5.3 collective-permute-start.16
  66.2 6.0 collective-permute-start.26
  77.9 5.6 collective-permute-start.28
  99.8 4.9 collective-permute-start.32
  124.1 5.1 collective-permute-start.37
  201.2 5.0 collective-permute-start.52
  211.8 5.0 collective-permute-start.54
  222.4 4.9 collective-permute-start.56
  320.4 5.0 collective-permute-start.77
  368.8 294.8 %while.18 = (s32[]{:T(128)}, f32[16,16,1024]{2,1,0:T(8,128)}, f32[1024]{0:T(1024)S(1)}, f32[16,16,1024]{2,1,0:T(8,128)}, f32[1,16,16,1024]{3,2,1,0:T(8,128)}, /*...) while((s32[]{:T(128)}, f32[16,16,1024]{2,1,0:T(8,128)}, ...), condition=%wide.region_7.8_spmd.clone, body=%wide.region_6.7_spmd.clone.sunk | while | flops 31996928 | bytes 124834800 | solution.py:155
  371.2 5.2 collective-permute-start.1
  378.3 7.9 fusion.502
  387.5 5.6 collective-permute-start.3
  397.7 5.8 collective-permute-start.5
  408.3 5.8 collective-permute-start.7
  419.4 5.8 collective-permute-start.9
  430.0 5.9 collective-permute-start.11
  440.7 5.8 collective-permute-start.13
  452.2 6.2 collective-permute-start.15
  460.4 6.6 fusion.516
  468.3 44.4 %gather_fusion = f32[1024]{0:T(1024)S(1)} fusion(f32[262144]{0:T(1024)} %bitcast.176, s32[1024]{0:T(1024)S(1)} %broadcast_clamp_fusion.2), kind=kCustom, calls=%fused_computation.clone.clone.1 | custom fusion | bytes 12288 | tf_op jit(solution)/shard_map/while/body/eval_jaxpr/jit(_take)/gather | solution.py:152
  521.7 7.9 fusion.502
  530.9 6.0 collective-permute-start.3
  541.6 6.8 collective-permute-start.5
  553.1 6.8 collective-permute-start.7
  564.7 7.6 collective-permute-start.9
  577.1 6.9 collective-permute-start.11
  588.7 7.1 collective-permute-start.13
  601.6 7.5 collective-permute-start.15
  611.0 6.6 fusion.516
  619.0 44.4 %gather_fusion = f32[1024]{0:T(1024)S(1)} fusion(f32[262144]{0:T(1024)} %bitcast.176, s32[1024]{0:T(1024)S(1)} %broadcast_clamp_fusion.2), kind=kCustom, calls=%fused_computation.clone.clone.1 | custom fusion | bytes 12288 | tf_op jit(solution)/shard_map/while/body/eval_jaxpr/jit(_take)/gather | solution.py:152
  668.5 6.1 collective-permute-start.88
  676.0 6.1 collective-permute-done.89
  682.2 6.2 collective-permute-start.90
  689.7 6.4 collective-permute-done.91
  696.2 6.5 collective-permute-start.92
  704.1 6.4 collective-permute-done.93
  710.6 6.1 collective-permute-start.94
  718.0 6.3 collective-permute-done.95
  724.4 6.9 collective-permute-start.96
  782.2 5.0 collective-permute-start.107
  792.8 5.0 collective-permute-start.109
  803.4 4.9 collective-permute-start.111
  835.0 5.0 collective-permute-start.117
  869.9 4.9 collective-permute-start.124
  901.6 5.0 collective-permute-start.130
  928.9 74.9 %psum.7 = f32[1024]{0:T(1024)S(1)} all-reduce(f32[1024]{0:T(1024)S(1)} %get-tuple-element.342), channel_id=1, replica_groups=mesh['period'=4,'slab'=32] {'period','slab'}, use_global_device_ids=true, to_apply=%region_10.11 | all-reduce | flops 1024 | bytes 8192 | tf_op jit(solution)/shard_map/psum | solution.py:161
  (422 shorter events, 582.1 us)
Async XLA Ops:
  1.5 12.4 %collective-permute-start.69 = (f32[1,16,1024]{2,1,0:T(8,128)S(1)}, f32[1,16,1024]{2,1,0:T(8,128)S(1)}, u32[]{:S(2)}, u32[]{:S(2)}) collective-permute-start(f32[1,16,1024]{2,1,0:T(8,128)S(1)} %get-tuple-element.468), channel_id=1, source_target_pairs={{0,1},{1,2},{2,3},{3,4},{4,5},{5,6},{6,7},{7,8},{8,9},{9,10},{10,1... | collective-permute-start | bytes 196616 | tf_op jit(solution)/shard_map/ppermute | solution.py:24
  5.0 8.9 collective-permute-start.70
  8.0 25.5 %collective-permute-start.17 = (f32[1,16,64]{2,1,0:T(8,128)S(1)}, f32[1,16,64]{2,1,0:T(8,128)S(1)}, u32[]{:S(2)}, u32[]{:S(2)}) collective-permute-start(f32[1,16,64]{2,1,0:T(8,128)S(1)} %bitcast_select_fusion.3), channel_id=1, source_target_pairs={{0,1},{1,2},{2,3},{3,4},{4,5},{5,6},{6,7},{7,8},{8,9},{9,10},{10,1... | collective-permute-start | bytes 12296 | tf_op jit(solution)/shard_map/ppermute | solution.py:24
  12.6 20.9 %collective-permute-start.19 = (f32[1,16,64]{2,1,0:T(8,128)S(1)}, f32[1,16,64]{2,1,0:T(8,128)S(1)}, u32[]{:S(2)}, u32[]{:S(2)}) collective-permute-start(f32[1,16,64]{2,1,0:T(8,128)S(1)} %bitcast_select_fusion.3), channel_id=1, source_target_pairs={{1,0},{2,1},{3,2},{4,3},{5,4},{6,5},{7,6},{8,7},{9,8},{10,9},{11,1... | collective-permute-start | bytes 12296 | tf_op jit(solution)/shard_map/ppermute | solution.py:25
  24.6 9.0 collective-permute-start.16
  66.2 7.4 collective-permute-start.26
  341.5 8.6 collective-permute-start.81
  352.0 7.3 collective-permute-start.83
  362.6 302.7 %collective-permute-start.85 = (f32[1,16,64]{2,1,0:T(8,128)S(1)}, f32[1,16,64]{2,1,0:T(8,128)S(1)}, u32[]{:S(2)}, u32[]{:S(2)}) collective-permute-start(f32[1,16,64]{2,1,0:T(8,128)S(1)} %fusion.306), channel_id=1, source_target_pairs={{0,1},{1,2},{2,3},{3,4},{4,5},{5,6},{6,7},{7,8},{8,9},{9,10},{10,1... | collective-permute-start | bytes 12296 | tf_op jit(solution)/shard_map/ppermute | solution.py:24
  367.5 297.8 %collective-permute-start.86 = (f32[1,16,64]{2,1,0:T(8,128)S(1)}, f32[1,16,64]{2,1,0:T(8,128)S(1)}, u32[]{:S(2)}, u32[]{:S(2)}) collective-permute-start(f32[1,16,64]{2,1,0:T(8,128)S(1)} %fusion.306), channel_id=1, source_target_pairs={{1,0},{2,1},{3,2},{4,3},{5,4},{6,5},{7,6},{8,7},{9,8},{10,9},{11,1... | collective-permute-start | bytes 12296 | tf_op jit(solution)/shard_map/ppermute | solution.py:25
  387.5 7.4 collective-permute-start.3
  396.4 7.4 collective-permute-start.4
  397.7 7.7 collective-permute-start.5
  407.0 7.8 collective-permute-start.6
  408.3 8.2 collective-permute-start.7
  418.1 7.4 collective-permute-start.8
  419.4 7.7 collective-permute-start.9
  428.7 7.5 collective-permute-start.10
  430.0 7.8 collective-permute-start.11
  439.4 7.4 collective-permute-start.12
  440.7 7.7 collective-permute-start.13
  450.9 7.9 collective-permute-start.14
  452.2 8.1 collective-permute-start.15
  529.6 7.6 collective-permute-start.2
  530.9 7.9 collective-permute-start.3
  540.3 8.4 collective-permute-start.4
  541.6 8.7 collective-permute-start.5
  551.8 8.4 collective-permute-start.6
  553.1 8.7 collective-permute-start.7
  563.4 9.6 collective-permute-start.8
  564.7 9.5 collective-permute-start.9
  575.8 8.5 collective-permute-start.10
  577.1 8.8 collective-permute-start.11
  587.4 9.3 collective-permute-start.12
  588.7 9.0 collective-permute-start.13
  600.3 9.1 collective-permute-start.14
  601.6 9.4 collective-permute-start.15
  668.5 7.5 collective-permute-start.88
  674.6 7.5 collective-permute-start.89
  682.2 7.5 collective-permute-start.90
  688.4 7.8 collective-permute-start.91
  696.2 7.9 collective-permute-start.92
  702.7 7.8 collective-permute-start.93
  710.6 7.5 collective-permute-start.94
  716.7 7.6 collective-permute-start.95
  724.4 8.3 collective-permute-start.96
  922.7 81.1 %collective-permute-start.134 = (f32[1,16,64]{2,1,0:T(8,128)S(1)}, f32[1,16,64]{2,1,0:T(8,128)S(1)}, u32[]{:S(2)}, u32[]{:S(2)}) collective-permute-start(f32[1,16,64]{2,1,0:T(8,128)S(1)} %fusion.447), channel_id=1, source_target_pairs={{0,1},{1,2},{2,3},{3,4},{4,5},{5,6},{6,7},{7,8},{8,9},{9,10},{10,1... | collective-permute-start | bytes 12296 | tf_op jit(solution)/shard_map/ppermute | solution.py:24
  927.6 76.2 %collective-permute-start.135 = (f32[1,16,64]{2,1,0:T(8,128)S(1)}, f32[1,16,64]{2,1,0:T(8,128)S(1)}, u32[]{:S(2)}, u32[]{:S(2)}) collective-permute-start(f32[1,16,64]{2,1,0:T(8,128)S(1)} %fusion.447), channel_id=1, source_target_pairs={{1,0},{2,1},{3,2},{4,3},{5,4},{6,5},{7,6},{8,7},{9,8},{10,9},{11,1... | collective-permute-start | bytes 12296 | tf_op jit(solution)/shard_map/ppermute | solution.py:25
  (123 other events, 1510.5 us)
where the time goes:
time: 1020 us; the launch traced here: 1010 us
  starting transfers between devices  493 us (48%)
  waiting for transfers between devices  273 us (27%)
  local copies, waits for them, and re-layouts  102 us (10%)
  blocking collectives  74.9 us (7%)
  other arithmetic  68.7 us (7%)
    ppermute x74, starting transfers between devices, with_halo(): before = lax.ppermute(last, axis, up)  389 us
    ppermute x74, waiting for transfers between devices, with_halo(): after = lax.ppermute(first, axis, down)  236 us
    ppermute x74, starting transfers between devices, with_halo(): after = lax.ppermute(first, axis, down)  95.6 us
    gather x2, local copies, waits for them, and re-layouts, advance(): jnp.take(dual_piezometric_level.reshape(-1), safe_index) * owned_mask  88.8 us
    psum x1, blocking collectives, shards(): grand_total = lax.psum(totals, ('period', 'slab'))  74.9 us
    mul x68, other arithmetic, relax(): return (source + nearby) * inverse  51.7 us
    ppermute x74, waiting for transfers between devices, with_halo(): before = lax.ppermute(last, axis, up)  26.9 us
  transfers between devices with their start and end apart: 154, of which 92 were waited for; matrix products, arithmetic and copies ran while one was open for 16% of the time, Pallas kernels for 0%

commit v1 on v0

v1 whole, which is shorter than its diff:
```python
import jax
import jax.numpy as jnp
from jax import lax
from jax.experimental import pallas as pl
from jax.experimental.pallas import tpu as pltpu
from jax.sharding import PartitionSpec as P

MESH = pl.DeviceIdType.MESH
F32 = jnp.float32
BF16 = jnp.bfloat16
STEPS = 2
SWEEPS = 8
CF = 16
X = 16
Z = 16
SLABS = 32
GROUPS = 4
W = 4
NR = X + 2 * W
NEX = STEPS * SWEEPS // W - 1
CY = 64
EXACT = lax.Precision.HIGHEST


def iota(shape, dim):
    return lax.broadcasted_iota(jnp.int32, shape, dim)


def y_below(v):
    rolled = pltpu.roll(v, 1, 2)
    return jnp.where(iota(v.shape, 2) == 0, pltpu.roll(rolled, 1, 1), rolled)


def y_above(v):
    rolled = pltpu.roll(v, 127, 2)
    return jnp.where(iota(v.shape, 2) == 127, pltpu.roll(rolled, 7, 1), rolled)


def z_below(v):
    return jnp.concatenate([v[:1], v[:-1]], 0)


def z_above(v):
    return jnp.concatenate([v[1:], v[-1:]], 0)


def cz_below(v):
    rolled = pltpu.roll(v, 1, 1)
    return jnp.where(iota(v.shape, 1) == 0, pltpu.roll(rolled, 64, 2), rolled)


def cz_above(v):
    rolled = pltpu.roll(v, 7, 1)
    return jnp.where(iota(v.shape, 1) == 7, pltpu.roll(rolled, 64, 2), rolled)


def device_of(group, row):
    return (2 * (group // 2) + row % 2, 2 * (row // 2) + group % 2)


def kernel(
    final_hbm, misfit_hbm, cond_hbm, cap_hbm, wells_ref, plan_ref,
    out_hbm, grad_ref,
    stage, condx, capx, misx, va, vb, co, inv, bi, own, rx,
    cbuf, ck, cco, cinv, cst, ga, gb, gbi, rs, pw, adv, planx, acc, sums, tot, st1, st2,
    ld_sem, ag_s, ag_r, sw_s, sw_r, id_s, id_r, hs_s, hs_r, ex_s, ex_r, e1_s, e1_r, e2_s, e2_r, own_s, own_r, out_sem,
):
    period = lax.axis_index("period")
    slab = lax.axis_index("slab")
    x_hi, core = period // 2, period % 2
    column, x_lo = slab // 2, slab % 2
    group = 2 * x_hi + x_lo
    row = 2 * column + core
    swapped = core != x_lo
    partner = (2 * x_hi + 1 - core, 2 * column + 1 - x_lo)
    far = (2 * (1 - x_hi) + core, 2 * column + 1 - x_lo)
    last = GROUPS - 1

    def load(k):
        src = (cond_hbm, cap_hbm, final_hbm, misfit_hbm)[k]
        return [
            pltpu.make_async_copy(src.at[:, :, pl.ds(128 * j, 128)], stage.at[k, :, :, j, :], ld_sem.at[k, j])
            for j in range(8)
        ]

    loads = [load(k) for k in range(4)]
    for group_of in loads:
        for copy in group_of:
            copy.start()

    barrier = pltpu.get_barrier_semaphore()

    def hello(device):
        pl.semaphore_signal(barrier, inc=1, device_id=device, device_id_type=MESH)

    def greet_slabs(k, c):
        hello((period, (slab + k) % SLABS))
        return c

    def greet_columns(k, c):
        hello((2 * x_hi + 1 - core, 2 * k + x_lo))
        return c

    lax.fori_loop(1, SLABS, greet_slabs, 0)
    lax.fori_loop(0, SLABS // 2, greet_columns, 0)
    for k in range(1, GROUPS):
        hello(device_of((group + k) % GROUPS, row))

    @pl.when(swapped)
    def _():
        hello(partner)

    fine_lane = iota((128, CY), 0)
    coarse_lane = iota((128, CY), 1)

    def restrict(block):
        rs[...] = jnp.sum(block, axis=0)
        total = jnp.zeros((Z, CY), F32)
        for s in range(8):
            pick = (coarse_lane == 8 * s + fine_lane // CF).astype(F32)
            total = total + jnp.dot(rs[:, s, :], pick, preferred_element_type=F32, precision=EXACT)
        total = total * (1.0 / (CF * CF))
        return jnp.concatenate([total[:8], total[8:]], axis=1)

    for k in range(3):
        for copy in loads[k]:
            copy.wait()
        cbuf[slab, k] = restrict(stage[k])

    pl.semaphore_wait(barrier, (SLABS - 1) + SLABS // 2 + GROUPS - 1 + swapped.astype(jnp.int32))

    def gather_copy(k, who):
        return pltpu.make_async_remote_copy(
            cbuf.at[who], cbuf.at[who], ag_s.at[k], ag_r.at[k],
            device_id=(period, (slab + k) % SLABS), device_id_type=MESH,
        )

    def gather_start(k, c):
        gather_copy(k, slab).start()
        return c

    lax.fori_loop(1, SLABS, gather_start, 0)
    for copy in loads[3]:
        copy.wait()

    body = pl.ds(W, X)

    def swap_copies(device):
        return [
            pltpu.make_async_remote_copy(
                stage.at[3], misx.at[body], sw_s.at[0], sw_r.at[0], device_id=device, device_id_type=MESH),
            pltpu.make_async_remote_copy(
                stage.at[0, pl.ds(0, 8)], condx.at[pl.ds(W + 1, 8)], sw_s.at[1], sw_r.at[1],
                device_id=device, device_id_type=MESH),
            pltpu.make_async_remote_copy(
                plan_ref, planx, sw_s.at[2], sw_r.at[2], device_id=device, device_id_type=MESH),
        ]

    def swap_final(device):
        return pltpu.make_async_remote_copy(
            stage.at[2], va.at[body], sw_s.at[3], sw_r.at[3], device_id=device, device_id_type=MESH)

    def far_copies(device):
        return [
            pltpu.make_async_remote_copy(
                stage.at[1], capx.at[body], id_s.at[0], id_r.at[0], device_id=device, device_id_type=MESH),
            pltpu.make_async_remote_copy(
                stage.at[0, pl.ds(8, 8)], condx.at[pl.ds(W + 9, 8)], id_s.at[1], id_r.at[1],
                device_id=device, device_id_type=MESH),
        ]

    below = device_of(group, row - 1 + SLABS * (row == 0))
    above = device_of(group, (row + 1) % SLABS)
    has_below = row > 0
    has_above = row < SLABS - 1

    def ghost_copies(side, with_start):
        if side == 0:
            device = below
            pairs = [(condx, pl.ds(W + 1, W + 1), pl.ds(W + 1 + X, W + 1))]
            cut, put = pl.ds(W, W), pl.ds(W + X, W)
        else:
            device = above
            pairs = [(condx, pl.ds(X, W + 1), pl.ds(0, W + 1))]
            cut, put = pl.ds(X, W), pl.ds(0, W)
        pairs += [(capx, cut, put), (misx, cut, put)]
        if with_start:
            pairs = [(va, cut, put)]
        return [
            pltpu.make_async_remote_copy(
                ref.at[a], ref.at[b], hs_s.at[side, n + 3 * with_start], hs_r.at[side, n + 3 * with_start],
                device_id=device, device_id_type=MESH)
            for n, (ref, a, b) in enumerate(pairs)
        ]

    def both_sides(act):
        @pl.when(has_below)
        def _():
            act(0)

        @pl.when(has_above)
        def _():
            act(1)

    def ghost_start():
        def act(side):
            for copy in ghost_copies(side, 0):
                copy.start()

            @pl.when(group == last)
            def _():
                ghost_copies(side, 1)[0].start()

        both_sides(act)

    @pl.when(swapped)
    def _():
        for copy in swap_copies(partner):
            copy.start()

        @pl.when((x_hi == 1) & (x_lo == 0))
        def _():
            swap_final(partner).start()

    @pl.when(jnp.logical_not(swapped))
    def _():
        for copy in far_copies(far):
            copy.start()

        def put(r, c):
            condx[W + 1 + r] = stage[0, r]
            capx[W + r] = stage[1, r]
            misx[W + r] = stage[3, r]
            return c

        lax.fori_loop(0, X, put, 0)
        planx[...] = plan_ref[...]

        @pl.when(group == last)
        def _():
            def put_final(r, c):
                va[W + r] = stage[2, r]
                return c

            lax.fori_loop(0, X, put_final, 0)

        ghost_start()

    def outside(lo_cond, lo):
        condx[pl.ds(lo_cond, W + 1)] = jnp.zeros((W + 1, Z, 8, 128), F32)
        capx[pl.ds(lo, W)] = jnp.ones((W, Z, 8, 128), F32)
        misx[pl.ds(lo, W)] = jnp.zeros((W, Z, 8, 128), F32)
        va[pl.ds(lo, W)] = jnp.zeros((W, Z, 8, 128), F32)

    @pl.when(jnp.logical_not(has_below))
    def _():
        outside(0, 0)

    @pl.when(jnp.logical_not(has_above))
    def _():
        outside(W + 1 + X, W + X)

    def gather_wait(k, c):
        gather_copy(k, (slab - k + SLABS) % SLABS).wait_recv()
        return c

    lax.fori_loop(1, SLABS, gather_wait, 0)
    nothing = jnp.zeros((8, 128), F32)
    for ref in (ck, ga, gb):
        ref[0] = nothing
        ref[SLABS + 1] = nothing

    def coarse_root(r, c):
        ck[r + 1] = jnp.sqrt(cbuf[r, 0])
        return c

    lax.fori_loop(0, SLABS, coarse_root, 0)
    CH = 8

    def chunk_rows(f):
        def step(n, c):
            f(n * CH)
            return c

        lax.fori_loop(0, SLABS // CH, step, 0)

    shape = (CH, 8, 128)

    def coarse_coefficients(r):
        k = ck[pl.ds(r + 1, CH)]
        column_of = iota(shape, 2) % CY
        layer = iota(shape, 1) + 8 * (iota(shape, 2) // CY)
        zero = jnp.zeros(shape, F32)
        scale = float(CF * CF)
        faces = [
            k * ck[pl.ds(r, CH)],
            k * ck[pl.ds(r + 2, CH)],
            jnp.where(column_of == 0, zero, k * pltpu.roll(k, 1, 2)),
            jnp.where(column_of == CY - 1, zero, k * pltpu.roll(k, 127, 2)),
            jnp.where(layer == 0, zero, scale * k * cz_below(k)),
            jnp.where(layer == Z - 1, zero, scale * k * cz_above(k)),
        ]
        store = cbuf[pl.ds(r, CH), 1] * float(CF * CF // STEPS)
        total = store
        for t in faces:
            total = total + t
        inverse = 1.0 / total
        for n in range(6):
            cco[n, pl.ds(r, CH)] = faces[n] * inverse
        cst[pl.ds(r, CH)] = store * inverse

    chunk_rows(coarse_coefficients)

    def coarse_sweep(src, dst):
        def rows(r):
            v = src[pl.ds(r + 1, CH)]
            c = pl.ds(r, CH)
            new = gbi[c] + cco[0, c] * src[pl.ds(r, CH)] + cco[1, c] * src[pl.ds(r + 2, CH)]
            new = new + (cco[2, c] * pltpu.roll(v, 1, 2) + cco[3, c] * pltpu.roll(v, 127, 2))
            new = new + (cco[4, c] * cz_below(v) + cco[5, c] * cz_above(v))
            dst[pl.ds(r + 1, CH)] = new

        chunk_rows(rows)

    def coarse_step():
        gbi[...] = cst[...] * ga[pl.ds(1, SLABS)]

        def pair(n, c):
            coarse_sweep(ga, gb)
            coarse_sweep(gb, ga)
            return c

        lax.fori_loop(0, SWEEPS // 2, pair, 0)

    ga[pl.ds(1, SLABS)] = cbuf[:, 2]

    def predict(n, c):
        coarse_step()
        return c

    lax.fori_loop(0, last - group, predict, 0)

    def extend(rows):
        flat = jnp.concatenate([part for c8 in rows for part in (c8[:, :CY], c8[:, CY:])], axis=0)
        for s in range(8):
            pick = (iota((CY, 128), 0) == 8 * s + iota((CY, 128), 1) // CF).astype(F32)
            wide = jnp.dot(flat, pick, preferred_element_type=F32, precision=EXACT)
            for n in range(len(rows)):
                pw[n, :, s, :] = wide[Z * n:Z * (n + 1)]

    @pl.when(group < last)
    def _():
        extend([ga[row], ga[row + 1], ga[row + 2]])
        for r in range(NR):
            va[r] = pw[0 if r < W else (1 if r < W + X else 2)]

    coarse_step()
    adv[...] = ga[row + 1]

    @pl.when(swapped)
    def _():
        for copy in swap_copies(partner) + far_copies(far):
            copy.wait_recv()

        @pl.when(group == last)
        def _():
            swap_final(partner).wait_recv()

        ghost_start()

    def ghost_wait(side):
        for copy in ghost_copies(1 - side, 0):
            copy.wait_recv()

        @pl.when(group == last)
        def _():
            ghost_copies(1 - side, 1)[0].wait_recv()

    both_sides(ghost_wait)

    def ghost_sent(side):
        for copy in ghost_copies(side, 0):
            copy.wait_send()

        @pl.when(group == last)
        def _():
            ghost_copies(side, 1)[0].wait_send()

    both_sides(ghost_sent)

    def root(r, c):
        condx[r] = jnp.sqrt(condx[r])
        return c

    lax.fori_loop(0, NR + 2, root, 0)
    fine = (Z, 8, 128)

    def coefficients(r, c):
        k = condx[r + 1]
        y = iota(fine, 1) * 128 + iota(fine, 2)
        zero = jnp.zeros(fine, F32)
        edge = jnp.zeros((1, 8, 128), F32)
        faces = [
            k * condx[r],
            k * condx[r + 2],
            jnp.where(y == 0, zero, k * y_below(k)),
            jnp.where(y == 1023, zero, k * y_above(k)),
            k * jnp.concatenate([edge, k[:-1]], 0),
            k * jnp.concatenate([k[1:], edge], 0),
        ]
        total = capx[r]
        for t in faces:
            total = total + t
        inverse = 1.0 / total
        inv[r] = inverse
        for n in range(6):
            co[n, r] = faces[n] * inverse
        return c

    lax.fori_loop(0, NR, coefficients, 0)

    def sweep(src, dst, lo, hi):
        def rows(r, c):
            v = src[r]
            new = (bi[r] + co[0, r] * src[r - 1]) + co[1, r] * src[r + 1]
            new = new + (co[4, r] * z_below(v) + co[5, r] * z_above(v))
            dst[r] = new + (co[2, r] * y_below(v) + co[3, r] * y_above(v))
            return c

        lax.fori_loop(lo, hi, rows, 0, unroll=2)

    def source(r, c):
        bi[r] = (capx[r] * va[r] + misx[r]) * inv[r]
        return c

    def sample(first):
        cell = wells_ref[...] - row * (X * Z * 1024)
        line = cell >> 7

        def part(n, c):
            v = va[pl.ds(W + 2 * n, 2)].reshape(256, 128)
            high = v.astype(BF16)
            rest = v - high.astype(F32)
            mid = rest.astype(BF16)
            low = (rest - mid.astype(F32)).astype(BF16)
            pieces = jnp.concatenate([high, mid, low], axis=1)
            hot = jnp.where(iota((256, 1024), 0) + 256 * n == line, 1.0, 0.0).astype(BF16)
            acc[...] += lax.dot_general(pieces, hot, (((0,), (0,)), ((), ())), preferred_element_type=F32)
            return c

        acc[...] = jnp.zeros(acc.shape, F32)
        lax.fori_loop(0, X // 2, part, 0)
        lines = acc[pl.ds(0, 128)] + acc[pl.ds(128, 128)] + acc[pl.ds(256, 128)]
        mine = jnp.where(iota((128, 1024), 0) == (cell & 127), lines, 0.0)
        got = jnp.sum(mine, axis=0, keepdims=True)
        sums[...] = got if first else sums[...] + got

    def exchange_copies(n, side):
        device, cut = (below, pl.ds(W, W)) if side == 0 else (above, pl.ds(X, W))
        return pltpu.make_async_remote_copy(
            va.at[cut], rx.at[n, 1 - side], ex_s.at[n, side], ex_r.at[n, 1 - side],
            device_id=device, device_id_type=MESH)

    per_step = SWEEPS // W
    for n in range(STEPS * per_step):
        if n % per_step == 0:
            lax.fori_loop(0, NR, source, 0)
        for k in range(1, W + 1):
            src, dst = (va, vb) if k % 2 else (vb, va)
            sweep(src, dst, k, NR - k)
        if n < NEX:
            both_sides(lambda side: exchange_copies(n, side).start())
        if n % per_step == per_step - 1:
            if n == STEPS * per_step - 1:
                @pl.when(swapped)
                def _():
                    own_copy = pltpu.make_async_remote_copy(
                        va.at[body], own, own_s, own_r, device_id=partner, device_id_type=MESH)
                    own_copy.start()
            sample(n // per_step == 0)
        if n < NEX:
            def arrive(side):
                exchange_copies(n, 1 - side).wait_recv()
                put = pl.ds(0, W) if side == 0 else pl.ds(W + X, W)
                va[put] = rx[n, side]
                exchange_copies(n, side).wait_send()

            both_sides(arrive)

    st1[group, 0] = restrict(va[body]) - adv[...]
    tot[...] = sums[...] * planx[...]
    for j in range(8):
        st1[group, 1, j:j + 1, :] = tot[:, 128 * j:128 * (j + 1)]

    def group_copy(k, who):
        return pltpu.make_async_remote_copy(
            st1.at[who], st1.at[who], e1_s.at[k], e1_r.at[k],
            device_id=device_of((group + k) % GROUPS, row), device_id_type=MESH)

    for k in range(1, GROUPS):
        group_copy(k, group).start()
    for k in range(1, GROUPS):
        group_copy(k, (group - k + GROUPS) % GROUPS).wait_recv()
    for g in range(1, GROUPS):
        st2[row, g - 1] = st1[g, 0]
    st2[row, 3] = (st1[0, 1] + st1[1, 1]) + (st1[2, 1] + st1[3, 1])

    def row_copy(k, who):
        return pltpu.make_async_remote_copy(
            st2.at[who], st2.at[who], e2_s.at[k], e2_r.at[k],
            device_id=device_of(group, (row + k) % SLABS), device_id_type=MESH)

    def row_start(k, c):
        row_copy(k, row).start()
        return c

    def row_wait(k, c):
        row_copy(k, (row - k + SLABS) % SLABS).wait_recv()
        return c

    lax.fori_loop(1, SLABS, row_start, 0)
    lax.fori_loop(1, SLABS, row_wait, 0)

    grad_ref[...] = jnp.sum(st2[:, 3], axis=0) * (1.0 / (STEPS * GROUPS))

    ga[pl.ds(1, SLABS)] = st2[:, 2]
    chain = last - period

    def correct(n, c):
        coarse_step()

        @pl.when(n < chain - 1)
        def _():
            ga[pl.ds(1, SLABS)] = ga[pl.ds(1, SLABS)] + st2[:, 1 - n]

        return c

    lax.fori_loop(0, chain, correct, 0)
    carried = jnp.where(chain > 0, 1.0, 0.0) * ga[slab + 1]
    extend([carried])

    @pl.when(swapped)
    def _():
        own_copy = pltpu.make_async_remote_copy(
            va.at[body], own, own_s, own_r, device_id=partner, device_id_type=MESH)
        own_copy.wait()

        def add(r, c):
            vb[W + r] = own[r] + pw[0]
            return c

        lax.fori_loop(0, X, add, 0)

    @pl.when(jnp.logical_not(swapped))
    def _():
        def add(r, c):
            vb[W + r] = va[W + r] + pw[0]
            return c

        lax.fori_loop(0, X, add, 0)

    outs = [
        pltpu.make_async_copy(vb.at[body, :, j, :], out_hbm.at[:, :, pl.ds(128 * j, 128)], out_sem.at[j])
        for j in range(8)
    ]
    for copy in outs:
        copy.start()

    def gather_sent(k, c):
        gather_copy(k, slab).wait_send()
        row_copy(k, row).wait_send()
        return c

    lax.fori_loop(1, SLABS, gather_sent, 0)
    for k in range(1, GROUPS):
        group_copy(k, group).wait_send()

    @pl.when(swapped)
    def _():
        for copy in swap_copies(partner):
            copy.wait_send()

        @pl.when((x_hi == 1) & (x_lo == 0))
        def _():
            swap_final(partner).wait_send()

    @pl.when(jnp.logical_not(swapped))
    def _():
        for copy in far_copies(far):
            copy.wait_send()

    for copy in outs:
        copy.wait()


def shards(final_level, misfit, conductivity, capacity, wells, plan):
    field = lambda *lead: pltpu.VMEM(lead + (Z, 8, 128), F32)
    tile = lambda *lead: pltpu.VMEM(lead + (8, 128), F32)
    dma = lambda *shape: pltpu.SemaphoreType.DMA(shape)
    vmem = pl.BlockSpec(memory_space=pltpu.VMEM)
    hbm = pl.BlockSpec(memory_space=pl.ANY)
    corrected, grad = pl.pallas_call(
        kernel,
        out_shape=(
            jax.ShapeDtypeStruct((X, Z, 1024), F32),
            jax.ShapeDtypeStruct((8, 128), F32),
        ),
        in_specs=[hbm, hbm, hbm, hbm, vmem, vmem],
        out_specs=(hbm, vmem),
        scratch_shapes=[
            field(4, X), field(NR + 2), field(NR), field(NR), field(NR), field(NR), field(6, NR), field(NR), field(NR),
            field(X), field(NEX, 2, W),
            tile(SLABS, 3), tile(SLABS + 2), tile(6, SLABS), tile(SLABS), tile(SLABS),
            tile(SLABS + 2), tile(SLABS + 2), tile(SLABS), field(), field(3), tile(),
            pltpu.VMEM((1, 1024), F32), pltpu.VMEM((384, 1024), F32), pltpu.VMEM((1, 1024), F32),
            pltpu.VMEM((1, 1024), F32), tile(GROUPS, 2), tile(SLABS, 4),
            dma(4, 8), dma(SLABS), dma(SLABS), dma(4), dma(4), dma(2), dma(2), dma(2, 4), dma(2, 4),
            dma(NEX, 2), dma(NEX, 2), dma(GROUPS), dma(GROUPS), dma(SLABS), dma(SLABS),
            pltpu.SemaphoreType.DMA, pltpu.SemaphoreType.DMA, dma(8),
        ],
        compiler_params=pltpu.CompilerParams(
            collective_id=0, has_side_effects=True, vmem_limit_bytes=60 * 2**20
        ),
    )(
        final_level, misfit[0], conductivity, capacity,
        wells.reshape(1, -1), plan.astype(F32),
    )
    return corrected[None], grad.reshape(-1)


def solution(mesh):
    return jax.shard_map(
        shards,
        mesh=mesh,
        in_specs=(
            P("slab", None, None),
            P("period", "slab", None, None),
            P("slab", None, None),
            P("slab", None, None),
            P(),
            P("period", None),
        ),
        out_specs=(P("period", "slab", None, None), P()),
        check_vma=False,
    )
```

time: 1020 us -> 141 us (0.14)
  the two profiles are of different devices: /device:TPU:0 before, /device:TPU:34 now
where the time goes in v1:
time: 141 us
  Pallas kernels  136 us (96%)
  local copies, waits for them, and re-layouts  2.91 us (2%)
    pallas_call x1, Pallas kernels, shards(): pl.pallas_call(kernel, out_shape=(jax.ShapeDtypeStruct((X, Z, 1024), F32)...  136 us
    unnamed x4, local copies, waits for them, and re-layouts  2.91 us

profile of v1, /device:TPU:34, one launch (start us, length us, event | category | flops | bytes accessed | tf_op | source)
XLA Modules:
  0.0 140.8 jit_solution(8666186350132267412)
XLA Ops:
  0.6 1.3 convert_element_type.3.plan_ref
  1.9 136.0 %shard_map.77 = (f32[16,16,1024]{2,1,0:T(8,128)}, f32[8,128]{1,0:T(8,128)}) custom-call(f32[16,16,1024]{2,1,0:T(8,128)} %final_hbm.1, f32[16,16,1024]{2,1,0:T(8,128)} %bitcast.5, f32[16,16,1024]{2,1,0:T(8,128)} %cond_hbm.1, f32[16,16,1024]{2,1,0:T(8,128)} %cap_hbm.1, s32[1,1024]{1,0:T(1,128)} %bitcast.7, f32[1,1024]{1,0:T(1,128)} %convert_element_type.3.plan_ref), custom_call_target="tpu_custom_call" | custom-call | tf_op jit(solution)/shard_map/pallas_call | solution.py:602
  137.9 0.0 copy-start
  137.9 2.3 %copy.10 = f32[1,16,16,1024]{3,2,1,0:T(8,128)} copy(f32[1,16,16,1024]{3,2,1,0:T(8,128)} %bitcast.4) | data formatting | bytes 2097152
  140.2 0.0 copy-done
  140.2 0.6 copy.11
Async XLA Ops:
  137.9 2.3 %copy-start = (f32[8,128]{1,0:T(8,128)S(1)}, f32[8,128]{1,0:T(8,128)}, u32[]{:S(2)}) copy-start(f32[8,128]{1,0:T(8,128)} %get-tuple-element.5) | copy-start | bytes 12292

commit v2 on v1

v2 whole, which is shorter than its diff:
```python
import jax
import jax.numpy as jnp
from jax import lax
from jax.experimental import pallas as pl
from jax.experimental.pallas import tpu as pltpu
from jax.sharding import PartitionSpec as P

MESH = pl.DeviceIdType.MESH
F32 = jnp.float32
BF16 = jnp.bfloat16
STEPS = 2
SWEEPS = 8
CF = 16
X = 16
Z = 16
SLABS = 32
GROUPS = 4
W = 4
NR = X + 2 * W
NEX = STEPS * SWEEPS // W - 1
CY = 64
EXACT = lax.Precision.HIGHEST


def iota(shape, dim):
    return lax.broadcasted_iota(jnp.int32, shape, dim)


def y_below(v):
    rolled = pltpu.roll(v, 1, 2)
    return jnp.where(iota(v.shape, 2) == 0, pltpu.roll(rolled, 1, 1), rolled)


def y_above(v):
    rolled = pltpu.roll(v, 127, 2)
    return jnp.where(iota(v.shape, 2) == 127, pltpu.roll(rolled, 7, 1), rolled)


LAYERS = [z for h in range(2) for z in range(h, Z, 2)]


def cz_both(v):
    turned = pltpu.roll(v, 64, 2)
    upper = iota(v.shape, 2) >= 64
    below = jnp.where(upper, turned, pltpu.roll(turned, 1, 1))
    above = jnp.where(upper, pltpu.roll(turned, 7, 1), turned)
    return below, above


def device_of(group, row):
    return (2 * (group // 2) + row % 2, 2 * (row // 2) + group % 2)


def kernel(
    final_hbm, misfit_hbm, cond_hbm, cap_hbm, wells_ref, plan_ref,
    out_hbm, grad_ref,
    stage, condx, capx, misx, va, vb, co, inv, bi, own, tx, rx,
    cbuf, crow, ck, cco, cst, ga, gb, gbi, rs, pw, fore, adv, planx, acc, sums, tot, st1, st2, st3,
    ld_sem, cr_s, cr_r, ag_s, ag_r, sw_s, sw_r, hs_s, hs_r, ex_s, ex_r, e1_s, e1_r, e2_s, e2_r, e3_s, e3_r,
    own_s, own_r, out_sem,
):
    period = lax.axis_index("period")
    slab = lax.axis_index("slab")
    x_hi, core = period // 2, period % 2
    column, x_lo = slab // 2, slab % 2
    group = 2 * x_hi + x_lo
    row = 2 * column + core
    swapped = core != x_lo
    partner = (2 * x_hi + 1 - core, 2 * column + 1 - x_lo)
    far = (2 * (1 - x_hi) + core, 2 * column + 1 - x_lo)
    last = GROUPS - 1

    def load(k):
        src = (cond_hbm, cap_hbm, final_hbm, misfit_hbm)[k]
        return [
            pltpu.make_async_copy(src.at[:, :, pl.ds(128 * j, 128)], stage.at[k, :, :, j, :], ld_sem.at[k, j])
            for j in range(8)
        ]

    loads = [load(k) for k in range(4)]
    for group_of in loads:
        for copy in group_of:
            copy.start()

    barrier = pltpu.get_barrier_semaphore()

    def hello(device):
        pl.semaphore_signal(barrier, inc=1, device_id=device, device_id_type=MESH)

    def greet(k, c):
        hello(device_of(group, (row + k) % SLABS))
        return c

    lax.fori_loop(1, SLABS, greet, 0)
    for k in range(1, GROUPS):
        hello(device_of((group + k) % GROUPS, row))

    @pl.when(swapped)
    def _():
        hello(partner)

    fine_lane = iota((128, CY), 0)
    coarse_lane = iota((128, CY), 1)

    def restrict(block):
        summed = jnp.sum(block, axis=0)
        rs[...] = jnp.concatenate([summed[z:z + 1] for z in LAYERS], axis=0)
        total = jnp.zeros((Z, CY), F32)
        for s in range(8):
            pick = (coarse_lane == 8 * s + fine_lane // CF).astype(F32)
            total = total + jnp.dot(rs[:, s, :], pick, preferred_element_type=F32, precision=EXACT)
        total = total * (1.0 / (CF * CF))
        return jnp.concatenate([total[:8], total[8:]], axis=1)

    for k in (0, 1, 2):
        for copy in loads[k]:
            copy.wait()
        crow[k] = restrict(stage[k])

    pl.semaphore_wait(barrier, (SLABS - 1) + GROUPS - 1 + swapped.astype(jnp.int32))

    def trade_rows():
        return pltpu.make_async_remote_copy(
            crow, cbuf.at[2 * column + x_lo], cr_s, cr_r, device_id=partner, device_id_type=MESH)

    def gather_copy(k, who):
        return pltpu.make_async_remote_copy(
            cbuf.at[who], cbuf.at[who], ag_s.at[k], ag_r.at[k],
            device_id=device_of(group, (row + k) % SLABS), device_id_type=MESH)

    def gather_start():
        def start(k, c):
            gather_copy(k, row).start()
            return c

        lax.fori_loop(1, SLABS, start, 0)

    body = pl.ds(W, X)

    def trade(k, ref, shift, n, lo, rows, device):
        return pltpu.make_async_remote_copy(
            stage.at[k, pl.ds(lo, rows)], ref.at[pl.ds(shift + lo, rows)], sw_s.at[n], sw_r.at[n],
            device_id=device, device_id_type=MESH)

    def trade_mis(d):
        return [trade(3, misx, W, 0, 0, W, d), trade(3, misx, W, 1, X - W, W, d)], [trade(3, misx, W, 2, W, X - 2 * W, d)]

    def trade_cap(d):
        return [trade(1, capx, W, 3, 0, W, d), trade(1, capx, W, 4, X - W, W, d)], [trade(1, capx, W, 5, W, X - 2 * W, d)]

    def trade_low(d):
        return [trade(0, condx, W + 1, 6, 0, W + 1, d)], [trade(0, condx, W + 1, 7, W + 1, X // 2 - W - 1, d)]

    def trade_high(d):
        return [trade(0, condx, W + 1, 8, X - W - 1, W + 1, d)], [trade(0, condx, W + 1, 9, X // 2, X // 2 - W - 1, d)]

    def trade_end(d):
        return [trade(2, va, W, 10, 0, W, d), trade(2, va, W, 11, X - W, W, d)], [trade(2, va, W, 12, W, X - 2 * W, d)]

    plan_copy = pltpu.make_async_remote_copy(
        plan_ref, planx, sw_s.at[13], sw_r.at[13], device_id=partner, device_id_type=MESH)
    to_last = (x_hi == 1) & (x_lo == 0)
    far_last = (x_hi == 0) & (x_lo == 0)

    def each(act, *lists):
        for part in range(2):
            for pair in lists:
                for copy in pair[part]:
                    act(copy)

    def outgoing(act):
        @pl.when(swapped & to_last)
        def _():
            each(act, trade_mis(partner), trade_end(partner))

        @pl.when(swapped & jnp.logical_not(to_last))
        def _():
            each(act, trade_mis(partner), trade_low(partner))

        @pl.when(swapped)
        def _():
            act(plan_copy)

        @pl.when(jnp.logical_not(swapped) & far_last)
        def _():
            each(act, trade_cap(far), trade_low(far), trade_high(far))

        @pl.when(jnp.logical_not(swapped) & jnp.logical_not(far_last))
        def _():
            each(act, trade_cap(far), trade_high(far))

    def incoming(part):
        for pair in (trade_cap(far), trade_high(far), trade_low(far), trade_mis(partner)):
            for copy in pair[part]:
                copy.wait_recv()

        @pl.when(group == last)
        def _():
            for copy in trade_end(partner)[part]:
                copy.wait_recv()

    below = device_of(group, (row + SLABS - 1) % SLABS)
    above = device_of(group, (row + 1) % SLABS)
    has_below = row > 0
    has_above = row < SLABS - 1

    def ghost_copies(side, with_start):
        if side == 0:
            device = below
            pairs = [(condx, pl.ds(W + 1, W + 1), pl.ds(W + 1 + X, W + 1))]
            cut, put = pl.ds(W, W), pl.ds(W + X, W)
        else:
            device = above
            pairs = [(condx, pl.ds(X, W + 1), pl.ds(0, W + 1))]
            cut, put = pl.ds(X, W), pl.ds(0, W)
        pairs += [(capx, cut, put), (misx, cut, put)]
        if with_start:
            pairs = [(va, cut, put)]
        return [
            pltpu.make_async_remote_copy(
                tx.at[side] if with_start else ref.at[a], ref.at[b],
                hs_s.at[side, n + 3 * with_start], hs_r.at[side, n + 3 * with_start],
                device_id=device, device_id_type=MESH)
            for n, (ref, a, b) in enumerate(pairs)
        ]

    def both_sides(act):
        @pl.when(has_below)
        def _():
            act(0)

        @pl.when(has_above)
        def _():
            act(1)

    def ghost_start():
        def act(side):
            for copy in ghost_copies(side, 0):
                copy.start()

            @pl.when(group == last)
            def _():
                tx[side] = va[pl.ds(W, W) if side == 0 else pl.ds(X, W)]
                ghost_copies(side, 1)[0].start()

        both_sides(act)

    def ghost_wait():
        def arrived(side):
            for copy in ghost_copies(1 - side, 0):
                copy.wait_recv()

            @pl.when(group == last)
            def _():
                ghost_copies(1 - side, 1)[0].wait_recv()

        both_sides(arrived)

    def ghost_sent():
        def act(side):
            for copy in ghost_copies(side, 0):
                copy.wait_send()

            @pl.when(group == last)
            def _():
                ghost_copies(side, 1)[0].wait_send()

        both_sides(act)

    fine = (Z, 8, 128)

    def coefficients(lo, hi):
        def one(r, c):
            k = jnp.sqrt(condx[r + 1])
            y = iota(fine, 1) * 128 + iota(fine, 2)
            zero = jnp.zeros(fine, F32)
            edge = jnp.zeros((1, 8, 128), F32)
            faces = [
                k * jnp.sqrt(condx[r]),
                k * jnp.sqrt(condx[r + 2]),
                jnp.where(y == 0, zero, k * y_below(k)),
                jnp.where(y == 1023, zero, k * y_above(k)),
                k * jnp.concatenate([edge, k[:-1]], 0),
                k * jnp.concatenate([k[1:], edge], 0),
            ]
            total = capx[r]
            for t in faces:
                total = total + t
            inverse = 1.0 / total
            inv[r] = inverse
            for n in range(6):
                co[n, r] = faces[n] * inverse
            return c

        lax.fori_loop(lo, hi, one, 0)

    for copy in loads[3]:
        copy.wait()

    @pl.when(swapped)
    def _():
        trade_rows().start()

    @pl.when(jnp.logical_not(swapped))
    def _():
        cbuf[row] = crow[...]
        gather_start()

    outgoing(lambda copy: copy.start())

    @pl.when(swapped)
    def _():
        pltpu.make_async_remote_copy(
            crow, cbuf.at[row], cr_s, cr_r, device_id=partner, device_id_type=MESH).wait_recv()
        gather_start()

    def outside(lo_cond, lo):
        condx[pl.ds(lo_cond, W + 1)] = jnp.zeros((W + 1, Z, 8, 128), F32)
        capx[pl.ds(lo, W)] = jnp.ones((W, Z, 8, 128), F32)
        misx[pl.ds(lo, W)] = jnp.zeros((W, Z, 8, 128), F32)
        va[pl.ds(lo, W)] = jnp.zeros((W, Z, 8, 128), F32)

    @pl.when(jnp.logical_not(has_below))
    def _():
        outside(0, 0)

    @pl.when(jnp.logical_not(has_above))
    def _():
        outside(W + 1 + X, W + X)

    @pl.when(jnp.logical_not(swapped))
    def _():
        def put(r, c):
            condx[W + 1 + r] = stage[0, r]
            capx[W + r] = stage[1, r]
            misx[W + r] = stage[3, r]
            return c

        lax.fori_loop(0, X, put, 0)
        planx[...] = plan_ref[...]

        @pl.when(group == last)
        def _():
            def put_final(r, c):
                va[W + r] = stage[2, r]
                return c

            lax.fori_loop(0, X, put_final, 0)

        ghost_start()

    def gather_wait(k, c):
        gather_copy(k, (row - k + SLABS) % SLABS).wait_recv()
        return c

    lax.fori_loop(1, SLABS, gather_wait, 0)
    nothing = jnp.zeros((8, 128), F32)
    for ref in (ck, ga, gb):
        ref[0] = nothing
        ref[SLABS + 1] = nothing

    def coarse_root(r, c):
        ck[r + 1] = jnp.sqrt(cbuf[r, 0])
        return c

    lax.fori_loop(0, SLABS, coarse_root, 0)
    CH = 8
    shape = (CH, 8, 128)

    def coarse_coefficients(r):
        k = ck[pl.ds(r + 1, CH)]
        column_of = iota(shape, 2) % CY
        layer = 2 * iota(shape, 1) + iota(shape, 2) // CY
        zero = jnp.zeros(shape, F32)
        scale = float(CF * CF)
        k_below, k_above = cz_both(k)
        faces = [
            k * ck[pl.ds(r, CH)],
            k * ck[pl.ds(r + 2, CH)],
            jnp.where(column_of == 0, zero, k * pltpu.roll(k, 1, 2)),
            jnp.where(column_of == CY - 1, zero, k * pltpu.roll(k, 127, 2)),
            jnp.where(layer == 0, zero, scale * k * k_below),
            jnp.where(layer == Z - 1, zero, scale * k * k_above),
        ]
        store = cbuf[pl.ds(r, CH), 1] * float(CF * CF // STEPS)
        total = store
        for t in faces:
            total = total + t
        inverse = 1.0 / total
        for n in range(6):
            cco[n, pl.ds(r, CH)] = faces[n] * inverse
        cst[pl.ds(r, CH)] = store * inverse

    for n in range(SLABS // CH):
        coarse_coefficients(n * CH)

    def coarse_sweep(src, dst):
        for n in range(SLABS // CH):
            r = n * CH
            v = src[pl.ds(r + 1, CH)]
            c = pl.ds(r, CH)
            v_below, v_above = cz_both(v)
            new = gbi[c] + cco[0, c] * src[pl.ds(r, CH)] + cco[1, c] * src[pl.ds(r + 2, CH)]
            new = new + (cco[2, c] * pltpu.roll(v, 1, 2) + cco[3, c] * pltpu.roll(v, 127, 2))
            dst[pl.ds(r + 1, CH)] = new + (cco[4, c] * v_below + cco[5, c] * v_above)

    def coarse_step():
        gbi[...] = cst[...] * ga[pl.ds(1, SLABS)]

        def pair(n, c):
            coarse_sweep(ga, gb)
            coarse_sweep(gb, ga)
            return c

        lax.fori_loop(0, SWEEPS // 2, pair, 0)

    @pl.when(swapped)
    def _():
        incoming(0)
        ghost_start()

    ga[pl.ds(1, SLABS)] = cbuf[:, 2]

    def predict(n, c):
        for k in range(3):
            fore[k] = ga[row + k]
        coarse_step()
        return c

    lax.fori_loop(0, last - group + 1, predict, 0)
    adv[...] = ga[row + 1]

    def extend(rows):
        flat = jnp.concatenate([part for c8 in rows for part in (c8[:, :CY], c8[:, CY:])], axis=0)
        for s in range(8):
            pick = (iota((CY, 128), 0) == 8 * s + iota((CY, 128), 1) // CF).astype(F32)
            wide = jnp.dot(flat, pick, preferred_element_type=F32, precision=EXACT)
            for n in range(len(rows)):
                pw[n, :, s, :] = wide[Z * n:Z * (n + 1)]

    def repeated(n):
        block = pw[n]
        places = [LAYERS.index(z) for z in range(Z)]
        return jnp.concatenate([block[p:p + 1] for p in places], axis=0)

    @pl.when(group < last)
    def _():
        extend([fore[0], fore[1], fore[2]])
        for part, (lo, hi) in enumerate(((0, W), (W, W + X), (W + X, NR))):
            rows = repeated(part)
            for r in range(lo, hi):
                va[r] = rows

    @pl.when(swapped)
    def _():
        incoming(1)
        plan_copy.wait_recv()

    coefficients(W + 1, W + X - 1)

    def sweep(src, dst, rows):
        for r in rows:
            for z in range(0, Z, 2):
                here = pl.ds(z, 2)
                v = src[r, here]
                if z == 0:
                    z_below = jnp.concatenate([v[:1], v[:1]], 0)
                else:
                    z_below = src[r, pl.ds(z - 1, 2)]
                if z == Z - 2:
                    z_above = jnp.concatenate([v[1:], v[1:]], 0)
                else:
                    z_above = src[r, pl.ds(z + 1, 2)]
                new = (bi[r, here] + co[0, r, here] * src[r - 1, here]) + co[1, r, here] * src[r + 1, here]
                new = new + (co[4, r, here] * z_below + co[5, r, here] * z_above)
                dst[r, here] = new + (co[2, r, here] * y_below(v) + co[3, r, here] * y_above(v))

    def source(lo, hi):
        def one(r, c):
            bi[r] = (capx[r] * va[r] + misx[r]) * inv[r]
            return c

        lax.fori_loop(lo, hi, one, 0)

    def sample():
        cell = wells_ref[...] - row * (X * Z * 1024)
        line = cell >> 7

        def part(n, c):
            v = va[pl.ds(W + 2 * n, 2)].reshape(256, 128)
            high = v.astype(BF16)
            rest = v - high.astype(F32)
            mid = rest.astype(BF16)
            low = (rest - mid.astype(F32)).astype(BF16)
            pieces = jnp.concatenate([high, mid, low], axis=1)
            hot = jnp.where(iota((256, 1024), 0) + 256 * n == line, 1.0, 0.0).astype(BF16)
            acc[...] += lax.dot_general(pieces, hot, (((0,), (0,)), ((), ())), preferred_element_type=F32)
            return c

        acc[...] = jnp.zeros(acc.shape, F32)
        lax.fori_loop(0, X // 2, part, 0)
        lines = acc[pl.ds(0, 128)] + acc[pl.ds(128, 128)] + acc[pl.ds(256, 128)]
        mine = jnp.where(iota((128, 1024), 0) == (cell & 127), lines, 0.0)
        sums[...] += jnp.sum(mine, axis=0, keepdims=True)

    def exchange_copy(n, side):
        return pltpu.make_async_remote_copy(
            tx.at[side], rx.at[n, 1 - side], ex_s.at[n, side], ex_r.at[n, 1 - side],
            device_id=below if side == 0 else above, device_id_type=MESH)

    sums[...] = jnp.zeros(sums.shape, F32)
    per_step = SWEEPS // W
    blocks = STEPS * per_step

    def block(n, c):
        opens = n % per_step == 0

        @pl.when(opens)
        def _():
            source(W + 1, W + X - 1)

        for k in range(1, W + 1):
            src, dst = (va, vb) if k % 2 else (vb, va)
            sweep(src, dst, range(W + k, W + X - k))

        @pl.when(n == 0)
        def _():
            ghost_wait()
            ghost_sent()
            coefficients(0, W + 1)
            coefficients(W + X - 1, NR)

        @pl.when(n > 0)
        def _():
            def arrive(side):
                exchange_copy(n - 1, 1 - side).wait_recv()
                va[pl.ds(0, W) if side == 0 else pl.ds(W + X, W)] = rx[n - 1, side]
                exchange_copy(n - 1, side).wait_send()

            both_sides(arrive)

        @pl.when(opens)
        def _():
            source(0, W + 1)
            source(W + X - 1, NR)

        for k in range(1, W + 1):
            src, dst = (va, vb) if k % 2 else (vb, va)
            sweep(src, dst, [*range(k, W + k), *range(W + X - k, NR - k)])

        @pl.when(n < blocks - 1)
        def _():
            tx[0] = va[pl.ds(W, W)]
            tx[1] = va[pl.ds(X, W)]
            both_sides(lambda side: exchange_copy(n, side).start())

        @pl.when((n % per_step == per_step - 1) & (n < blocks - 1))
        def _():
            sample()

        return c

    lax.fori_loop(0, blocks, block, 0)

    st1[group] = restrict(va[body]) - adv[...]

    def group_copy(ref, send, receive, k, who):
        return pltpu.make_async_remote_copy(
            ref.at[who], ref.at[who], send.at[k], receive.at[k],
            device_id=device_of((group + k) % GROUPS, row), device_id_type=MESH)

    def group_start(*how):
        for k in range(1, GROUPS):
            group_copy(*how, k, group).start()

    def group_wait(*how):
        for k in range(1, GROUPS):
            group_copy(*how, k, (group - k + GROUPS) % GROUPS).wait_recv()

    group_start(st1, e1_s, e1_r)
    own_copy = pltpu.make_async_remote_copy(
        va.at[body], own, own_s, own_r, device_id=partner, device_id_type=MESH)
    @pl.when(swapped)
    def _():
        own_copy.start()

    sample()
    tot[...] = sums[...] * planx[...]
    for j in range(8):
        st2[row, 3, j:j + 1, :] = tot[:, 128 * j:128 * (j + 1)]
    group_wait(st1, e1_s, e1_r)
    for g in range(1, GROUPS):
        st2[row, g - 1] = st1[g]

    def row_copy(k, who):
        return pltpu.make_async_remote_copy(
            st2.at[who], st2.at[who], e2_s.at[k], e2_r.at[k],
            device_id=device_of(group, (row + k) % SLABS), device_id_type=MESH)

    def row_start(k, c):
        row_copy(k, row).start()
        return c

    def row_wait(k, c):
        row_copy(k, (row - k + SLABS) % SLABS).wait_recv()
        return c

    lax.fori_loop(1, SLABS, row_start, 0)
    lax.fori_loop(1, SLABS, row_wait, 0)
    st3[group] = jnp.sum(st2[:, 3], axis=0)
    group_start(st3, e3_s, e3_r)

    ga[pl.ds(1, SLABS)] = st2[:, 2]
    chain = last - period

    def correct(n, c):
        coarse_step()

        @pl.when(n < chain - 1)
        def _():
            ga[pl.ds(1, SLABS)] = ga[pl.ds(1, SLABS)] + st2[:, 1 - n]

        return c

    lax.fori_loop(0, chain, correct, 0)
    carried = jnp.where(chain > 0, 1.0, 0.0) * ga[slab + 1]
    extend([carried])
    wide = repeated(0)

    @pl.when(swapped)
    def _():
        own_copy.wait()
        for r in range(X):
            vb[W + r] = own[r] + wide

    @pl.when(jnp.logical_not(swapped))
    def _():
        for r in range(X):
            vb[W + r] = va[W + r] + wide

    outs = [
        pltpu.make_async_copy(vb.at[body, :, j, :], out_hbm.at[:, :, pl.ds(128 * j, 128)], out_sem.at[j])
        for j in range(8)
    ]
    for copy in outs:
        copy.start()
    group_wait(st3, e3_s, e3_r)
    grad_ref[...] = ((st3[0] + st3[1]) + (st3[2] + st3[3])) * (1.0 / (STEPS * GROUPS))

    def rows_sent(k, c):
        gather_copy(k, row).wait_send()
        row_copy(k, row).wait_send()
        return c

    lax.fori_loop(1, SLABS, rows_sent, 0)
    for k in range(1, GROUPS):
        group_copy(st1, e1_s, e1_r, k, group).wait_send()
        group_copy(st3, e3_s, e3_r, k, group).wait_send()
    outgoing(lambda copy: copy.wait_send())

    @pl.when(swapped)
    def _():
        trade_rows().wait_send()

    for copy in outs:
        copy.wait()


def shards(final_level, misfit, conductivity, capacity, wells, plan):
    field = lambda *lead: pltpu.VMEM(lead + (Z, 8, 128), F32)
    tile = lambda *lead: pltpu.VMEM(lead + (8, 128), F32)
    dma = lambda *shape: pltpu.SemaphoreType.DMA(shape)
    vmem = pl.BlockSpec(memory_space=pltpu.VMEM)
    hbm = pl.BlockSpec(memory_space=pl.ANY)
    corrected, grad = pl.pallas_call(
        kernel,
        out_shape=(
            jax.ShapeDtypeStruct((X, Z, 1024), F32),
            jax.ShapeDtypeStruct((8, 128), F32),
        ),
        in_specs=[hbm, hbm, hbm, hbm, vmem, vmem],
        out_specs=(hbm, vmem),
        scratch_shapes=[
            field(4, X), field(NR + 2), field(NR), field(NR), field(NR), field(NR), field(6, NR), field(NR), field(NR),
            field(X), field(2, W), field(NEX, 2, W),
            tile(SLABS, 3), tile(3), tile(SLABS + 2), tile(6, SLABS), tile(SLABS),
            tile(SLABS + 2), tile(SLABS + 2), tile(SLABS), field(), field(3), tile(3), tile(),
            pltpu.VMEM((1, 1024), F32), pltpu.VMEM((384, 1024), F32), pltpu.VMEM((1, 1024), F32),
            pltpu.VMEM((1, 1024), F32), tile(GROUPS), tile(SLABS, 4), tile(GROUPS),
            dma(4, 8), pltpu.SemaphoreType.DMA, pltpu.SemaphoreType.DMA, dma(SLABS), dma(SLABS),
            dma(14), dma(14), dma(2, 4), dma(2, 4), dma(NEX, 2), dma(NEX, 2),
            dma(GROUPS), dma(GROUPS), dma(SLABS), dma(SLABS), dma(GROUPS), dma(GROUPS),
            pltpu.SemaphoreType.DMA, pltpu.SemaphoreType.DMA, dma(8),
        ],
        compiler_params=pltpu.CompilerParams(
            collective_id=0, has_side_effects=True, vmem_limit_bytes=60 * 2**20
        ),
    )(
        final_level, misfit[0], conductivity, capacity,
        wells.reshape(1, -1), plan.astype(F32),
    )
    return corrected[None], grad.reshape(-1)


def solution(mesh):
    return jax.shard_map(
        shards,
        mesh=mesh,
        in_specs=(
            P("slab", None, None),
            P("period", "slab", None, None),
            P("slab", None, None),
            P("slab", None, None),
            P(),
            P("period", None),
        ),
        out_specs=(P("period", "slab", None, None), P()),
        check_vma=False,
    )
```

time: 141 us -> 91 us (0.65)
  the two profiles are of different devices: /device:TPU:34 before, /device:TPU:0 now
where the time goes in v2:
time: 91 us; the launch traced here: 90.8 us
  Pallas kernels  85.9 us (94%)
  local copies, waits for them, and re-layouts  2.91 us (3%)
  other arithmetic  1.28 us (1%)
    pallas_call x1, Pallas kernels, shards(): pl.pallas_call(kernel, out_shape=(jax.ShapeDtypeStruct((X, Z, 1024), F32)...  85.9 us
    unnamed x4, local copies, waits for them, and re-layouts  2.91 us

profile of v2, /device:TPU:0, one launch (start us, length us, event | category | flops | bytes accessed | tf_op | source)
XLA Modules:
  0.0 90.8 jit_solution(5190030074052093876)
XLA Ops:
  0.6 1.3 %convert_element_type.3.plan_ref = f32[1,1024]{1,0:T(1,128)} convert(s32[1,1024]{1,0:T(1,128)} %param.11) | non-fusion elementwise | flops 1024 | bytes 8192 | tf_op jit(solution)/shard_map/convert_element_type | solution.py:700
  1.9 85.9 %shard_map.77 = (f32[16,16,1024]{2,1,0:T(8,128)}, f32[8,128]{1,0:T(8,128)}) custom-call(f32[16,16,1024]{2,1,0:T(8,128)} %final_hbm.1, f32[16,16,1024]{2,1,0:T(8,128)} %bitcast.5, f32[16,16,1024]{2,1,0:T(8,128)} %cond_hbm.1, f32[16,16,1024]{2,1,0:T(8,128)} %cap_hbm.1, s32[1,1024]{1,0:T(1,128)} %bitcast.7, f32[1,1024]{1,0:T(1,128)} %convert_element_type.3.plan_ref), custom_call_target="tpu_custom_call" | custom-call | tf_op jit(solution)/shard_map/pallas_call | solution.py:675
  87.9 0.0 copy-start
  87.9 2.3 %copy.10 = f32[1,16,16,1024]{3,2,1,0:T(8,128)} copy(f32[1,16,16,1024]{3,2,1,0:T(8,128)} %bitcast.4) | data formatting | bytes 2097152
  90.2 0.0 copy-done
  90.2 0.6 copy.11
Async XLA Ops:
  87.9 2.3 %copy-start = (f32[8,128]{1,0:T(8,128)S(1)}, f32[8,128]{1,0:T(8,128)}, u32[]{:S(2)}) copy-start(f32[8,128]{1,0:T(8,128)} %get-tuple-element.5) | copy-start | bytes 12292

commit v3 on v2

--- a/solution.py
+++ b/solution.py
@@ -55,7 +55,7 @@
     final_hbm, misfit_hbm, cond_hbm, cap_hbm, wells_ref, plan_ref,
     out_hbm, grad_ref,
     stage, condx, capx, misx, va, vb, co, inv, bi, own, tx, rx,
-    cbuf, crow, ck, cco, cst, ga, gb, gbi, rs, pw, fore, adv, planx, acc, sums, tot, st1, st2, st3,
+    cbuf, crow, ck, cco, cst, ga, gb, gbi, rs, pw, fore, adv, plan_row, planx, rootx, acc, sums, tot, st1, st2, st3,
     ld_sem, cr_s, cr_r, ag_s, ag_r, sw_s, sw_r, hs_s, hs_r, ex_s, ex_r, e1_s, e1_r, e2_s, e2_r, e3_s, e3_r,
     own_s, own_r, out_sem,
 ):
@@ -99,24 +99,22 @@
     def _():
         hello(partner)
 
-    fine_lane = iota((128, CY), 0)
-    coarse_lane = iota((128, CY), 1)
-
-    def restrict(block):
-        summed = jnp.sum(block, axis=0)
-        rs[...] = jnp.concatenate([summed[z:z + 1] for z in LAYERS], axis=0)
-        total = jnp.zeros((Z, CY), F32)
-        for s in range(8):
-            pick = (coarse_lane == 8 * s + fine_lane // CF).astype(F32)
-            total = total + jnp.dot(rs[:, s, :], pick, preferred_element_type=F32, precision=EXACT)
-        total = total * (1.0 / (CF * CF))
-        return jnp.concatenate([total[:8], total[8:]], axis=1)
-
-    for k in (0, 1, 2):
+    def restrict(*blocks):
+        for n, block in enumerate(blocks):
+            summed = jnp.sum(block, axis=0)
+            rs[pl.ds(Z * n, Z)] = jnp.concatenate([summed[z:z + 1] for z in LAYERS], axis=0)
+        rows = Z * len(blocks)
+        flat = jnp.concatenate([rs[pl.ds(0, rows), s, :] for s in range(8)], axis=1)
+        pick = (iota((1024, CY), 1) == iota((1024, CY), 0) // CF).astype(F32)
+        total = jnp.dot(flat, pick, preferred_element_type=F32, precision=EXACT) * (1.0 / (CF * CF))
+        return [
+            jnp.concatenate([total[Z * n:Z * n + 8], total[Z * n + 8:Z * n + Z]], axis=1)
+            for n in range(len(blocks))
+        ]
+
+    for k in (0, 1):
         for copy in loads[k]:
             copy.wait()
-        crow[k] = restrict(stage[k])
-
     pl.semaphore_wait(barrier, (SLABS - 1) + GROUPS - 1 + swapped.astype(jnp.int32))
 
     def trade_rows():
@@ -158,41 +156,44 @@
         return [trade(2, va, W, 10, 0, W, d), trade(2, va, W, 11, X - W, W, d)], [trade(2, va, W, 12, W, X - 2 * W, d)]
 
     plan_copy = pltpu.make_async_remote_copy(
-        plan_ref, planx, sw_s.at[13], sw_r.at[13], device_id=partner, device_id_type=MESH)
+        plan_row, planx, sw_s.at[13], sw_r.at[13], device_id=partner, device_id_type=MESH)
     to_last = (x_hi == 1) & (x_lo == 0)
     far_last = (x_hi == 0) & (x_lo == 0)
 
-    def each(act, *lists):
-        for part in range(2):
-            for pair in lists:
-                for copy in pair[part]:
-                    act(copy)
-
-    def outgoing(act):
+    def in_order(*lists):
+        return [copy for pairs in lists for part in range(2) for pair in pairs for copy in pair[part]]
+
+    HEAD = 2
+
+    def outgoing(act, lo=0, hi=None):
         @pl.when(swapped & to_last)
         def _():
-            each(act, trade_mis(partner), trade_end(partner))
+            for copy in in_order([trade_cap(partner)], [trade_mis(partner)])[lo:hi]:
+                act(copy)
 
         @pl.when(swapped & jnp.logical_not(to_last))
         def _():
-            each(act, trade_mis(partner), trade_low(partner))
-
-        @pl.when(swapped)
-        def _():
-            act(plan_copy)
+            for copy in in_order([trade_low(partner)], [trade_mis(partner)])[lo:hi]:
+                act(copy)
 
         @pl.when(jnp.logical_not(swapped) & far_last)
         def _():
-            each(act, trade_cap(far), trade_low(far), trade_high(far))
+            for copy in in_order([trade_low(far), trade_high(far)], [trade_end(far)])[lo:hi]:
+                act(copy)
 
         @pl.when(jnp.logical_not(swapped) & jnp.logical_not(far_last))
         def _():
-            each(act, trade_cap(far), trade_high(far))
-
-    def incoming(part):
-        for pair in (trade_cap(far), trade_high(far), trade_low(far), trade_mis(partner)):
+            for copy in in_order([trade_cap(far), trade_high(far)])[lo:hi]:
+                act(copy)
+
+    def incoming_data(part):
+        for pair in (trade_cap(far), trade_high(far), trade_low(far)):
             for copy in pair[part]:
                 copy.wait_recv()
+
+    def incoming_source(part):
+        for copy in trade_mis(partner)[part]:
+            copy.wait_recv()
 
         @pl.when(group == last)
         def _():
@@ -204,24 +205,22 @@
     has_below = row > 0
     has_above = row < SLABS - 1
 
-    def ghost_copies(side, with_start):
-        if side == 0:
-            device = below
-            pairs = [(condx, pl.ds(W + 1, W + 1), pl.ds(W + 1 + X, W + 1))]
-            cut, put = pl.ds(W, W), pl.ds(W + X, W)
-        else:
-            device = above
-            pairs = [(condx, pl.ds(X, W + 1), pl.ds(0, W + 1))]
-            cut, put = pl.ds(X, W), pl.ds(0, W)
-        pairs += [(capx, cut, put), (misx, cut, put)]
-        if with_start:
-            pairs = [(va, cut, put)]
+    def ghost_copies(side, names):
+        device = below if side == 0 else above
+        cut, put = (pl.ds(W, W), pl.ds(W + X, W)) if side == 0 else (pl.ds(X, W), pl.ds(0, W))
+        wide_cut, wide_put = (
+            (pl.ds(W + 1, W + 1), pl.ds(W + 1 + X, W + 1)) if side == 0 else (pl.ds(X, W + 1), pl.ds(0, W + 1)))
+        table = {
+            "cond": (0, condx.at[wide_cut], condx.at[wide_put]),
+            "cap": (1, capx.at[cut], capx.at[put]),
+            "mis": (2, misx.at[cut], misx.at[put]),
+            "end": (3, tx.at[side], va.at[put]),
+        }
         return [
             pltpu.make_async_remote_copy(
-                tx.at[side] if with_start else ref.at[a], ref.at[b],
-                hs_s.at[side, n + 3 * with_start], hs_r.at[side, n + 3 * with_start],
+                table[name][1], table[name][2], hs_s.at[side, table[name][0]], hs_r.at[side, table[name][0]],
                 device_id=device, device_id_type=MESH)
-            for n, (ref, a, b) in enumerate(pairs)
+            for name in names
         ]
 
     def both_sides(act):
@@ -233,80 +232,112 @@
         def _():
             act(1)
 
-    def ghost_start():
+    DATA = ("cond", "cap")
+
+    def ghost_data():
         def act(side):
-            for copy in ghost_copies(side, 0):
+            for copy in ghost_copies(side, DATA):
                 copy.start()
+
+        both_sides(act)
+
+    def ghost_source():
+        def act(side):
+            ghost_copies(side, ["mis"])[0].start()
 
             @pl.when(group == last)
             def _():
                 tx[side] = va[pl.ds(W, W) if side == 0 else pl.ds(X, W)]
-                ghost_copies(side, 1)[0].start()
+                ghost_copies(side, ["end"])[0].start()
 
         both_sides(act)
 
-    def ghost_wait():
+    def ghost_wait(names):
         def arrived(side):
-            for copy in ghost_copies(1 - side, 0):
+            for copy in ghost_copies(1 - side, names):
                 copy.wait_recv()
+
+        both_sides(arrived)
+
+    def ghost_sent():
+        def act(side):
+            for copy in ghost_copies(side, (*DATA, "mis")):
+                copy.wait_send()
 
             @pl.when(group == last)
             def _():
-                ghost_copies(1 - side, 1)[0].wait_recv()
-
-        both_sides(arrived)
-
-    def ghost_sent():
-        def act(side):
-            for copy in ghost_copies(side, 0):
-                copy.wait_send()
-
-            @pl.when(group == last)
-            def _():
-                ghost_copies(side, 1)[0].wait_send()
+                ghost_copies(side, ["end"])[0].wait_send()
 
         both_sides(act)
 
     fine = (Z, 8, 128)
 
-    def coefficients(lo, hi):
-        def one(r, c):
-            k = jnp.sqrt(condx[r + 1])
-            y = iota(fine, 1) * 128 + iota(fine, 2)
-            zero = jnp.zeros(fine, F32)
-            edge = jnp.zeros((1, 8, 128), F32)
-            faces = [
-                k * jnp.sqrt(condx[r]),
-                k * jnp.sqrt(condx[r + 2]),
-                jnp.where(y == 0, zero, k * y_below(k)),
-                jnp.where(y == 1023, zero, k * y_above(k)),
-                k * jnp.concatenate([edge, k[:-1]], 0),
-                k * jnp.concatenate([k[1:], edge], 0),
-            ]
-            total = capx[r]
-            for t in faces:
-                total = total + t
-            inverse = 1.0 / total
-            inv[r] = inverse
-            for n in range(6):
-                co[n, r] = faces[n] * inverse
+    def roots(lo, hi):
+        for r in range(lo, hi):
+            rootx[r] = jnp.sqrt(condx[r])
+
+    def coefficients(r):
+        k = rootx[r + 1]
+        y = iota(fine, 1) * 128 + iota(fine, 2)
+        zero = jnp.zeros(fine, F32)
+        edge = jnp.zeros((1, 8, 128), F32)
+        faces = [
+            k * rootx[r],
+            k * rootx[r + 2],
+            jnp.where(y == 0, zero, k * y_below(k)),
+            jnp.where(y == 1023, zero, k * y_above(k)),
+            k * jnp.concatenate([edge, k[:-1]], 0),
+            k * jnp.concatenate([k[1:], edge], 0),
+        ]
+        total = capx[r]
+        for t in faces:
+            total = total + t
+        inverse = 1.0 / total
+        inv[r] = inverse
+        for n in range(6):
+            co[n, r] = faces[n] * inverse
+
+    def inner_coefficients():
+        roots(W + 1, W + 1 + X)
+
+        def pair(n, c):
+            coefficients(W + 1 + 2 * n)
+            coefficients(W + 2 + 2 * n)
             return c
 
-        lax.fori_loop(lo, hi, one, 0)
+        lax.fori_loop(0, (X - 2) // 2, pair, 0)
+
+    def outer_coefficients():
+        roots(0, W + 1)
+        roots(W + 1 + X, NR + 2)
+
+        def pair(n, c):
+            coefficients(n)
+            coefficients(W + X - 1 + n)
+            return c
+
+        lax.fori_loop(0, W + 1, pair, 0)
+
+    outgoing(lambda copy: copy.start(), 0, HEAD)
+    for copy in loads[2]:
+        copy.wait()
+    for k, rows in enumerate(restrict(stage[0], stage[1], stage[2])):
+        crow[k] = rows
+    plan_row[...] = plan_ref[...].astype(F32)
+
+    @pl.when(swapped)
+    def _():
+        trade_rows().start()
+        plan_copy.start()
 
     for copy in loads[3]:
         copy.wait()
-
-    @pl.when(swapped)
-    def _():
-        trade_rows().start()
+    outgoing(lambda copy: copy.start(), HEAD)
 
     @pl.when(jnp.logical_not(swapped))
     def _():
         cbuf[row] = crow[...]
         gather_start()
-
-    outgoing(lambda copy: copy.start())
 
     @pl.when(swapped)
     def _():
@@ -337,7 +368,7 @@
             return c
 
         lax.fori_loop(0, X, put, 0)
-        planx[...] = plan_ref[...]
+        planx[...] = plan_row[...]
 
         @pl.when(group == last)
         def _():
@@ -347,7 +378,8 @@
 
             lax.fori_loop(0, X, put_final, 0)
 
-        ghost_start()
+        ghost_data()
+        ghost_source()
 
     def gather_wait(k, c):
         gather_copy(k, (row - k + SLABS) % SLABS).wait_recv()
@@ -416,8 +448,8 @@
 
     @pl.when(swapped)
     def _():
-        incoming(0)
-        ghost_start()
+        incoming_data(0)
+        ghost_data()
 
     ga[pl.ds(1, SLABS)] = cbuf[:, 2]
 
@@ -432,11 +464,11 @@
 
     def extend(rows):
         flat = jnp.concatenate([part for c8 in rows for part in (c8[:, :CY], c8[:, CY:])], axis=0)
+        pick = (iota((CY, 1024), 0) == iota((CY, 1024), 1) // CF).astype(F32)
+        wide = jnp.dot(flat, pick, preferred_element_type=F32, precision=EXACT)
         for s in range(8):
-            pick = (iota((CY, 128), 0) == 8 * s + iota((CY, 128), 1) // CF).astype(F32)
-            wide = jnp.dot(flat, pick, preferred_element_type=F32, precision=EXACT)
             for n in range(len(rows)):
-                pw[n, :, s, :] = wide[Z * n:Z * (n + 1)]
+                pw[n, :, s, :] = wide[Z * n:Z * (n + 1), 128 * s:128 * (s + 1)]
 
     def repeated(n):
         block = pw[n]
@@ -453,10 +485,22 @@
 
     @pl.when(swapped)
     def _():
-        incoming(1)
+        incoming_data(1)
+
+    inner_coefficients()
+
+    @pl.when(swapped)
+    def _():
+        incoming_source(0)
+        ghost_source()
+
+    ghost_wait(DATA)
+    outer_coefficients()
+
+    @pl.when(swapped)
+    def _():
+        incoming_source(1)
         plan_copy.wait_recv()
-
-    coefficients(W + 1, W + X - 1)
 
     def sweep(src, dst, rows):
         for r in rows:
@@ -476,11 +520,8 @@
                 dst[r, here] = new + (co[2, r, here] * y_below(v) + co[3, r, here] * y_above(v))
 
     def source(lo, hi):
-        def one(r, c):
-            bi[r] = (capx[r] * va[r] + misx[r]) * inv[r]
-            return c
-
-        lax.fori_loop(lo, hi, one, 0)
+        rows = pl.ds(lo, hi - lo)
+        bi[rows] = (capx[rows] * va[rows] + misx[rows]) * inv[rows]
 
     def sample():
         cell = wells_ref[...] - row * (X * Z * 1024)
@@ -489,17 +530,15 @@
         def part(n, c):
             v = va[pl.ds(W + 2 * n, 2)].reshape(256, 128)
             high = v.astype(BF16)
-            rest = v - high.astype(F32)
-            mid = rest.astype(BF16)
-            low = (rest - mid.astype(F32)).astype(BF16)
-            pieces = jnp.concatenate([high, mid, low], axis=1)
+            low = (v - high.astype(F32)).astype(BF16)
+            pieces = jnp.concatenate([high, low], axis=1)
             hot = jnp.where(iota((256, 1024), 0) + 256 * n == line, 1.0, 0.0).astype(BF16)
             acc[...] += lax.dot_general(pieces, hot, (((0,), (0,)), ((), ())), preferred_element_type=F32)
             return c
 
         acc[...] = jnp.zeros(acc.shape, F32)
         lax.fori_loop(0, X // 2, part, 0)
-        lines = acc[pl.ds(0, 128)] + acc[pl.ds(128, 128)] + acc[pl.ds(256, 128)]
+        lines = acc[pl.ds(0, 128)] + acc[pl.ds(128, 128)]
         mine = jnp.where(iota((128, 1024), 0) == (cell & 127), lines, 0.0)
         sums[...] += jnp.sum(mine, axis=0, keepdims=True)
 
@@ -525,10 +564,13 @@
 
         @pl.when(n == 0)
         def _():
-            ghost_wait()
+            ghost_wait(["mis"])
+
+            @pl.when(group == last)
+            def _():
+                ghost_wait(["end"])
+
             ghost_sent()
-            coefficients(0, W + 1)
-            coefficients(W + X - 1, NR)
 
         @pl.when(n > 0)
         def _():
@@ -562,7 +604,7 @@
 
     lax.fori_loop(0, blocks, block, 0)
 
-    st1[group] = restrict(va[body]) - adv[...]
+    st1[group] = restrict(va[body])[0] - adv[...]
 
     def group_copy(ref, send, receive, k, who):
         return pltpu.make_async_remote_copy(
@@ -661,6 +703,7 @@
     @pl.when(swapped)
     def _():
         trade_rows().wait_send()
+        plan_copy.wait_send()
 
     for copy in outs:
         copy.wait()
@@ -684,8 +727,8 @@
             field(4, X), field(NR + 2), field(NR), field(NR), field(NR), field(NR), field(6, NR), field(NR), field(NR),
             field(X), field(2, W), field(NEX, 2, W),
             tile(SLABS, 3), tile(3), tile(SLABS + 2), tile(6, SLABS), tile(SLABS),
-            tile(SLABS + 2), tile(SLABS + 2), tile(SLABS), field(), field(3), tile(3), tile(),
-            pltpu.VMEM((1, 1024), F32), pltpu.VMEM((384, 1024), F32), pltpu.VMEM((1, 1024), F32),
+            tile(SLABS + 2), tile(SLABS + 2), tile(SLABS), tile(3 * Z), field(3), tile(3), tile(),
+            pltpu.VMEM((1, 1024), F32), pltpu.VMEM((1, 1024), F32), field(NR + 2), pltpu.VMEM((256, 1024), F32), pltpu.VMEM((1, 1024), F32),
             pltpu.VMEM((1, 1024), F32), tile(GROUPS), tile(SLABS, 4), tile(GROUPS),
             dma(4, 8), pltpu.SemaphoreType.DMA, pltpu.SemaphoreType.DMA, dma(SLABS), dma(SLABS),
             dma(14), dma(14), dma(2, 4), dma(2, 4), dma(NEX, 2), dma(NEX, 2),
@@ -697,7 +740,7 @@
         ),
     )(
         final_level, misfit[0], conductivity, capacity,
-        wells.reshape(1, -1), plan.astype(F32),
+        wells.reshape(1, -1), plan,
     )
     return corrected[None], grad.reshape(-1)
 

time: 91 us -> 83 us (0.912)
  Pallas kernels: 85.9 us -> 79.2 us
  other arithmetic: 1.28 us -> 0 us
    pallas_call x1, Pallas kernels: 85.9 us -> 79.2 us  [shards(): pl.pallas_call(kernel, out_shape=(jax.ShapeDtypeStruct((X, Z, 1024), F32)...]
    convert_element_type x1 -> x0, other arithmetic: 1.28 us -> none  [shards(): plan.astype(F32)]
where the time goes in v3:
time: 83 us; the launch traced here: 82.8 us
  Pallas kernels  79.2 us (95%)
  local copies, waits for them, and re-layouts  2.91 us (4%)
    pallas_call x1, Pallas kernels, shards(): pl.pallas_call(kernel, out_shape=(jax.ShapeDtypeStruct((X, Z, 1024), F32)...  79.2 us
    unnamed x4, local copies, waits for them, and re-layouts  2.91 us

profile of v3, /device:TPU:0, one launch (start us, length us, event | category | flops | bytes accessed | tf_op | source)
XLA Modules:
  0.0 82.8 jit_solution(8052380838357144983)
XLA Ops:
  0.6 79.2 %shard_map.77 = (f32[16,16,1024]{2,1,0:T(8,128)}, f32[8,128]{1,0:T(8,128)}) custom-call(f32[16,16,1024]{2,1,0:T(8,128)} %final_hbm.1, f32[16,16,1024]{2,1,0:T(8,128)} %bitcast.5, f32[16,16,1024]{2,1,0:T(8,128)} %cond_hbm.1, f32[16,16,1024]{2,1,0:T(8,128)} %cap_hbm.1, s32[1,1024]{1,0:T(1,128)} %bitcast.7, s32[1,1024]{1,0:T(1,128)} %plan_ref.1), custom_call_target="tpu_custom_call" | custom-call | tf_op jit(solution)/shard_map/pallas_call | solution.py:718
  79.9 0.0 copy-start
  79.9 2.3 %copy.10 = f32[1,16,16,1024]{3,2,1,0:T(8,128)} copy(f32[1,16,16,1024]{3,2,1,0:T(8,128)} %bitcast.4) | data formatting | bytes 2097152
  82.2 0.0 copy-done
  82.2 0.6 copy.11
Async XLA Ops:
  79.9 2.3 %copy-start = (f32[8,128]{1,0:T(8,128)S(1)}, f32[8,128]{1,0:T(8,128)}, u32[]{:S(2)}) copy-start(f32[8,128]{1,0:T(8,128)} %get-tuple-element.5) | copy-start | bytes 12292

commit v4 on v3

--- a/solution.py
+++ b/solution.py
@@ -572,29 +572,41 @@
 
             ghost_sent()
 
-        @pl.when(n > 0)
-        def _():
-            def arrive(side):
+        def outer(side):
+            has = has_below if side == 0 else has_above
+            put = pl.ds(0, W) if side == 0 else pl.ds(W + X, W)
+
+            @pl.when((n > 0) & has)
+            def _():
                 exchange_copy(n - 1, 1 - side).wait_recv()
-                va[pl.ds(0, W) if side == 0 else pl.ds(W + X, W)] = rx[n - 1, side]
+                va[put] = rx[n - 1, side]
                 exchange_copy(n - 1, side).wait_send()
 
-            both_sides(arrive)
-
-        @pl.when(opens)
-        def _():
-            source(0, W + 1)
-            source(W + X - 1, NR)
-
-        for k in range(1, W + 1):
-            src, dst = (va, vb) if k % 2 else (vb, va)
-            sweep(src, dst, [*range(k, W + k), *range(W + X - k, NR - k)])
-
-        @pl.when(n < blocks - 1)
-        def _():
-            tx[0] = va[pl.ds(W, W)]
-            tx[1] = va[pl.ds(X, W)]
-            both_sides(lambda side: exchange_copy(n, side).start())
+            @pl.when(opens)
+            def _():
+                if side == 0:
+                    source(0, W + 1)
+                else:
+                    source(W + X - 1, NR)
+
+            for k in range(1, W + 1):
+                src, dst = (va, vb) if k % 2 else (vb, va)
+                sweep(src, dst, range(k, W + k) if side == 0 else range(W + X - k, NR - k))
+
+            @pl.when((n < blocks - 1) & has)
+            def _():
+                tx[side] = va[pl.ds(W, W) if side == 0 else pl.ds(X, W)]
+                exchange_copy(n, side).start()
+
+        @pl.when(core == 0)
+        def _():
+            outer(1)
+            outer(0)
+
+        @pl.when(core == 1)
+        def _():
+            outer(0)
+            outer(1)
 
         @pl.when((n % per_step == per_step - 1) & (n < blocks - 1))
         def _():
@@ -629,30 +641,44 @@
     sample()
     tot[...] = sums[...] * planx[...]
     for j in range(8):
-        st2[row, 3, j:j + 1, :] = tot[:, 128 * j:128 * (j + 1)]
+        st2[core, column, 3, j:j + 1, :] = tot[:, 128 * j:128 * (j + 1)]
     group_wait(st1, e1_s, e1_r)
     for g in range(1, GROUPS):
-        st2[row, g - 1] = st1[g]
-
-    def row_copy(k, who):
+        st2[core, column, g - 1] = st1[g]
+
+    CHIPS = SLABS // 2
+
+    def chip_copy(k, who):
         return pltpu.make_async_remote_copy(
-            st2.at[who], st2.at[who], e2_s.at[k], e2_r.at[k],
-            device_id=device_of(group, (row + k) % SLABS), device_id_type=MESH)
-
-    def row_start(k, c):
-        row_copy(k, row).start()
-        return c
-
-    def row_wait(k, c):
-        row_copy(k, (row - k + SLABS) % SLABS).wait_recv()
-        return c
-
-    lax.fori_loop(1, SLABS, row_start, 0)
-    lax.fori_loop(1, SLABS, row_wait, 0)
-    st3[group] = jnp.sum(st2[:, 3], axis=0)
+            st2.at[core, who], st2.at[core, who], e2_s.at[k], e2_r.at[k],
+            device_id=device_of(group, 2 * ((column + k) % CHIPS) + core), device_id_type=MESH)
+
+    def chip_start(k, c):
+        chip_copy(k, column).start()
+        return c
+
+    def chip_wait(k, c):
+        chip_copy(k, (column - k + CHIPS) % CHIPS).wait_recv()
+        return c
+
+    def pair_copy(who):
+        return pltpu.make_async_remote_copy(
+            st2.at[who], st2.at[who], e2_s.at[0], e2_r.at[0],
+            device_id=device_of(group, 2 * column + 1 - core), device_id_type=MESH)
+
+    lax.fori_loop(1, CHIPS, chip_start, 0)
+    lax.fori_loop(1, CHIPS, chip_wait, 0)
+    pair_copy(core).start()
+    pair_copy(1 - core).wait_recv()
+
+    def jumps(k):
+        return [(2 * chip + odd, st2[odd, chip, k]) for chip in range(CHIPS) for odd in range(2)]
+
+    st3[group] = jnp.sum(st2[0, :, 3], axis=0) + jnp.sum(st2[1, :, 3], axis=0)
     group_start(st3, e3_s, e3_r)
 
-    ga[pl.ds(1, SLABS)] = st2[:, 2]
+    for r, rows in jumps(2):
+        ga[1 + r] = rows
     chain = last - period
 
     def correct(n, c):
@@ -660,7 +686,8 @@
 
         @pl.when(n < chain - 1)
         def _():
-            ga[pl.ds(1, SLABS)] = ga[pl.ds(1, SLABS)] + st2[:, 1 - n]
+            for r, rows in jumps(1 - n):
+                ga[1 + r] = ga[1 + r] + rows
 
         return c
 
@@ -691,10 +718,15 @@
 
     def rows_sent(k, c):
         gather_copy(k, row).wait_send()
-        row_copy(k, row).wait_send()
+        return c
+
+    def chips_sent(k, c):
+        chip_copy(k, column).wait_send()
         return c
 
     lax.fori_loop(1, SLABS, rows_sent, 0)
+    lax.fori_loop(1, CHIPS, chips_sent, 0)
+    pair_copy(core).wait_send()
     for k in range(1, GROUPS):
         group_copy(st1, e1_s, e1_r, k, group).wait_send()
         group_copy(st3, e3_s, e3_r, k, group).wait_send()
@@ -729,7 +761,7 @@
             tile(SLABS, 3), tile(3), tile(SLABS + 2), tile(6, SLABS), tile(SLABS),
             tile(SLABS + 2), tile(SLABS + 2), tile(SLABS), tile(3 * Z), field(3), tile(3), tile(),
             pltpu.VMEM((1, 1024), F32), pltpu.VMEM((1, 1024), F32), field(NR + 2), pltpu.VMEM((256, 1024), F32), pltpu.VMEM((1, 1024), F32),
-            pltpu.VMEM((1, 1024), F32), tile(GROUPS), tile(SLABS, 4), tile(GROUPS),
+            pltpu.VMEM((1, 1024), F32), tile(GROUPS), tile(2, SLABS // 2, 4), tile(GROUPS),
             dma(4, 8), pltpu.SemaphoreType.DMA, pltpu.SemaphoreType.DMA, dma(SLABS), dma(SLABS),
             dma(14), dma(14), dma(2, 4), dma(2, 4), dma(NEX, 2), dma(NEX, 2),
             dma(GROUPS), dma(GROUPS), dma(SLABS), dma(SLABS), dma(GROUPS), dma(GROUPS),

time: 83 us -> 81.7 us (0.984); the launches traced: 82.8 us -> 80.3 us
  Pallas kernels: 79.2 us -> 76.7 us
    pallas_call x1, Pallas kernels: 79.2 us -> 76.7 us  [shards(): pl.pallas_call(kernel, out_shape=(jax.ShapeDtypeStruct((X, Z, 1024), F32)...]
where the time goes in v4:
time: 81.7 us; the launch traced here: 80.3 us
  Pallas kernels  76.7 us (94%)
  local copies, waits for them, and re-layouts  2.91 us (4%)
    pallas_call x1, Pallas kernels, shards(): pl.pallas_call(kernel, out_shape=(jax.ShapeDtypeStruct((X, Z, 1024), F32)...  76.7 us
    unnamed x4, local copies, waits for them, and re-layouts  2.91 us

profile of v4, /device:TPU:0, one launch (start us, length us, event | category | flops | bytes accessed | tf_op | source)
XLA Modules:
  0.0 80.3 jit_solution(1314707386063315647)
XLA Ops:
  0.6 76.7 %shard_map.77 = (f32[16,16,1024]{2,1,0:T(8,128)}, f32[8,128]{1,0:T(8,128)}) custom-call(f32[16,16,1024]{2,1,0:T(8,128)} %final_hbm.1, f32[16,16,1024]{2,1,0:T(8,128)} %bitcast.5, f32[16,16,1024]{2,1,0:T(8,128)} %cond_hbm.1, f32[16,16,1024]{2,1,0:T(8,128)} %cap_hbm.1, s32[1,1024]{1,0:T(1,128)} %bitcast.7, s32[1,1024]{1,0:T(1,128)} %plan_ref.1), custom_call_target="tpu_custom_call" | custom-call | tf_op jit(solution)/shard_map/pallas_call | solution.py:750
  77.4 0.0 copy-start
  77.4 2.3 %copy.10 = f32[1,16,16,1024]{3,2,1,0:T(8,128)} copy(f32[1,16,16,1024]{3,2,1,0:T(8,128)} %bitcast.4) | data formatting | bytes 2097152
  79.7 0.0 copy-done
  79.7 0.6 copy.11
Async XLA Ops:
  77.4 2.3 %copy-start = (f32[8,128]{1,0:T(8,128)S(1)}, f32[8,128]{1,0:T(8,128)}, u32[]{:S(2)}) copy-start(f32[8,128]{1,0:T(8,128)} %get-tuple-element.5) | copy-start | bytes 12292
